TPU v7x, 32 devices: a whole 2x2x4 slice. The times are simulated.
32 devices in a mesh: macro: 8 (over z, y), pool: 4 (over x, core).
Axes of the slice: x: 2, y: 2, z: 4, core: 2. Of those that a mesh axis runs over, the one named last changes fastest.
Arguments:
- history: float32 [729, 16384], P(None, ('macro', 'pool')), may hold values from -6 to 6
- yield_flags: int32 [729, 16384], P(None, ('macro', 'pool')), may hold values 0 or 1
- strain: float32 [6, 16384], P(None, ('macro', 'pool')), may hold values from -6 to 6
- qp_to_rve: int32 [32, 512], P(('macro', 'pool')), may hold values from 0 to 511, each once within a row
- new_owner: int32 [16384, 1], P(('macro', 'pool')), may hold values from 0 to 31; in each aligned block of 512 rows (0 to 511, 512 to 1023, ...) at most 32 rows name the same one
- stiffness: float32 [9, 9, 81, 81], replicated, as said below
- pattern: int32 [9, 9], replicated, may hold values from 0 to 1, as said below
- coupling: float32 [3, 6, 729], replicated, as said below
- plastic_dir: float32 [3, 729], replicated, may hold values from -6 to 6
Outputs:
- new_history: float32 [729, 32768], P(None, ('macro', 'pool'))
- stress: float32 [6, 16384], P(None, ('macro', 'pool'))
Inputs may be any that keep to these rules, and one draw needn't show every extreme that they name: `new_owner`: among the rows of one device no owner is named more than 32 times, a bound that some block reaches. `qp_to_rve`: each row is a permutation of 0 to 511. `pattern`: Symmetric, with ones on the diagonal. stiffness[a, b] is the transpose of stiffness[b, a]; diagonal entries of diagonal blocks lie in 0.5 to 1.5, all others in 0 to 0.032. `coupling`: entries lie in -5.7 to 6.3.
All inputs are finite; a program needn't handle non-finite values. No bound on the sum of `yield_flags` on one device may be relied on, other than what follows from the above.
Results may differ from a plain program's by a relative error of at most 0.0003.
Values sent between devices are 32-bit elements; how exact they have to be, the bound alone decides.
No kernel may reach another device: no remote copies, remote signals or barrier semaphores. Data moves between devices by JAX's collectives and lax.ppermute only.
A program may use at most 128 MiB of HBM per device.

v0:
```python
import functools
import math

import jax
import jax.numpy as jnp
from jax import lax
from jax.experimental import pallas as pl
from jax.experimental.pallas import tpu as pltpu
from jax.sharding import PartitionSpec as P

ITERS = 3
LANES = 128
PLANES = 4
PATTERN = 32

NN = (((1,), (0,)), ((), ()))
NT = (((1,), (1,)), ((), ()))
TN = (((0,), (0,)), ((), ()))


def up(value, unit):
    return -(-value // unit) * unit


def dot(a, b, dims=NN):
    return lax.dot_general(a, b, dims, preferred_element_type=jnp.float32)


def halves(x):
    hi = x.astype(jnp.bfloat16)
    lo = (x - hi.astype(jnp.float32)).astype(jnp.bfloat16)
    return hi, lo


def whereabouts(devices):
    me = lax.axis_index("macro") * lax.axis_size("pool") + lax.axis_index("pool")
    lanes = devices // PLANES
    return me, me // lanes, me % lanes, lanes


def hot(row, count):
    rows = lax.broadcasted_iota(jnp.int32, (count, row.shape[1]), 0)
    return jnp.where(rows == row, 1.0, 0.0).astype(jnp.bfloat16)


def pack_kernel(coupling, plastic, strain, owner, qp, pattern, small):
    top = 0
    for c in range(coupling.shape[0]):
        small[top:top + coupling.shape[1], :] = coupling[c]
        top += coupling.shape[1]
    for part in (plastic, strain, owner, qp):
        small[top:top + part.shape[0], 0:part.shape[1]] = part[...].astype(jnp.float32)
        top += part.shape[0]
    count = pattern.shape[0]
    for a in range(count):
        for b in range(count):
            couples = jnp.full((1, LANES), pattern[a, b].astype(jnp.float32))
            small[PATTERN + a * count + b:PATTERN + a * count + b + 1, 0:LANES] = couples


def prep_kernel(devices, per_peer, comps, voigt, *refs):
    sources, outs, (kfull, pad), local, sem = refs[:4], refs[4:13], refs[13:15], refs[15:19], refs[19]
    khi, klo, hist_s, weight_s, strain_s, place_s, qp_s, cstack, pdir = outs
    small, stiff, hist, flag = local
    copies = [
        pltpu.make_async_copy(source, target, sem.at[i])
        for i, (source, target) in enumerate(zip(sources, local))
    ]
    for copy in copies:
        copy.start()
    nodes, columns = hist.shape
    nb, blk = stiff.shape[0], stiff.shape[2]
    at_plastic = comps * voigt
    at_strain = at_plastic + comps
    at_owner = at_strain + voigt
    copies[0].wait()

    me, plane, lane, lanes = whereabouts(devices)
    owner = small[at_owner:at_owner + 1, 0:columns].astype(jnp.int32)
    apart = owner // lanes ^ plane
    target = owner % lanes
    away = target ^ lane
    shifted = away % 2 * (lanes // 2) + away // 2
    turn = jnp.where(apart == 2, 0, jnp.where(apart == 1, 1, jnp.where(apart == 3, 2, 3)))
    key = turn * lanes + jnp.where((apart == 2) | (apart == 1), shifted, target)
    key_ids = lax.broadcasted_iota(jnp.int32, (devices, columns), 0)
    mine = jnp.where(key_ids == key, 1.0, 0.0)
    earlier = jnp.where(
        lax.broadcasted_iota(jnp.int32, (columns, columns), 0)
        < lax.broadcasted_iota(jnp.int32, (columns, columns), 1), 1.0, 0.0
    ).astype(jnp.bfloat16)
    before = dot(mine.astype(jnp.bfloat16), earlier)
    rank = jnp.sum(before * mine, axis=0, keepdims=True)
    tally = jnp.sum(mine, axis=1, keepdims=True)
    ahead = jnp.where(key_ids < key, tally, 0.0)
    position = (rank + jnp.sum(ahead, axis=0, keepdims=True)).astype(jnp.int32)

    order = hot(position, columns)
    pad[...] = jnp.zeros_like(pad)
    pad[0:1, :] = key.astype(jnp.float32)
    pad[1:2, :] = rank
    placed = dot(pad[...].astype(jnp.bfloat16), order, NT)
    place_s[...] = jnp.broadcast_to(
        (placed[0:1, :] * per_peer + placed[1:2, :]).astype(jnp.int32), place_s.shape
    )

    pad[0:1, :] = (position // 256).astype(jnp.float32)
    pad[1:2, :] = (position % 256).astype(jnp.float32)
    found = dot(pad[...].astype(jnp.bfloat16), hot(small[at_owner + 1:at_owner + 2, 0:columns].astype(jnp.int32), columns))
    at = (found[0:1, :] * 256.0 + found[1:2, :]).astype(jnp.int32)
    qp_s[...] = jnp.broadcast_to(at, qp_s.shape)
    pad[...] = jnp.zeros_like(pad)
    pad[0:voigt, :] = small[at_strain:at_owner, 0:columns]
    hi, lo = halves(pad[...])
    serves = hot(at, columns)
    strain_s[...] = dot(hi, serves, NT) + dot(lo, serves, NT)

    kfull[...] = jnp.zeros_like(kfull)
    copies[1].wait()
    for a in range(nb):
        for b in range(nb):
            kfull[a * blk:(a + 1) * blk, b * blk:(b + 1) * blk] = (
                stiff[a, b] * small[PATTERN + a * nb + b:PATTERN + a * nb + b + 1, 0:blk]
            )
    k = kfull[...]
    kh = k.astype(jnp.bfloat16)
    khi[...] = kh
    klo[...] = (k - kh.astype(jnp.float32)).astype(jnp.bfloat16)

    copies[2].wait()
    copies[3].wait()
    hi, lo = halves(hist[...])
    hist_s[...] = jnp.zeros_like(hist_s)
    hist_s[0:nodes, :] = dot(hi, order, NT) + dot(lo, order, NT)
    h = hist_s[...]
    weight_s[...] = jnp.zeros_like(weight_s)
    weight_s[0:nodes, :] = dot(flag[...].astype(jnp.float32).astype(jnp.bfloat16), order, NT)
    weight_s[...] = weight_s[...] * h * h / (1.0 + h * h)

    cstack[...] = jnp.zeros_like(cstack)
    for c in range(comps):
        cpl = small[c * voigt:(c + 1) * voigt, :]
        hi = cpl.astype(jnp.bfloat16).astype(jnp.float32)
        cstack[c, 0:voigt, 0:nodes] = hi
        cstack[c, 8:8 + voigt, 0:nodes] = hi
        cstack[c, 16:16 + voigt, 0:nodes] = cpl - hi
    pdir[...] = jnp.zeros_like(pdir)
    for c in range(comps):
        spread = jnp.broadcast_to(small[at_plastic + c:at_plastic + c + 1, :], (LANES, nodes))
        pdir[c, 0:nodes, :] = jnp.transpose(spread)


def sweep(rows, comps, span):
    pieces = 4 * span // LANES
    cuts = [rows // 16 * i // pieces * 16 for i in range(pieces + 1)]
    for top, end in zip(cuts, cuts[1:]):
        for c in range(comps):
            yield slice(top, end), slice(c * span, (c + 1) * span), c


def fold(x):
    return jnp.sum(x.reshape(x.shape[0] // 8, 8, x.shape[1]), axis=0)


def total(parts):
    return jnp.sum(parts, axis=0, keepdims=True)


def solve_kernel(scale, first, earlier, khi, klo, hist, weight, strain, cstack, pdir, place, *refs):
    earlier_updated, refs = refs[:earlier], refs[earlier:]
    updated, stress, blocks = refs[0], refs[1], refs[2:-5]
    field, resid, image, solved, split = refs[-5:]
    rows, span = hist.shape
    comps = pdir.shape[0]
    wide = comps * span
    zero = jnp.zeros((8, span), jnp.float32)

    def flow(c, r):
        return jnp.concatenate([pdir[c, r, :]] * (span // LANES), axis=1)

    def keep(r, c, x):
        split[r, c * span:(c + 1) * span], split[r, wide + c * span:wide + (c + 1) * span] = (
            halves(x)
        )

    s = strain[...]
    s_hi = s.astype(jnp.bfloat16).astype(jnp.float32)
    s3 = jnp.concatenate([s_hi, s - s_hi, s_hi, jnp.zeros_like(s)], axis=0).astype(jnp.bfloat16)
    split[rows:, :] = jnp.zeros((split.shape[0] - rows, 2 * wide), jnp.bfloat16)
    for c in range(comps):
        image[:, c * span:(c + 1) * span] = dot(cstack[c].astype(jnp.bfloat16), s3, TN)
    parts = zero
    for r, l, c in sweep(rows, comps, span):
        d = image[r, l] - weight[r, :] * hist[r, :] * flow(c, r)
        resid[r, l] = d
        field[r, l] = d
        keep(r, c, d)
        parts = parts + fold(d * d)
    norm = total(parts)
    for step in range(ITERS):
        both = dot(khi[...], split[...])
        image[...] = both[:, 0:wide] + both[:, wide:] + dot(klo[...], split[:, 0:wide])
        parts = zero
        for r, l, c in sweep(rows, comps, span):
            d = field[r, l]
            q = image[r, l] + (1.5 - weight[r, :]) * d
            image[r, l] = q
            parts = parts + fold(d * q)
        alpha = norm / jnp.maximum(total(parts), 1.0)
        if step == ITERS - 1:
            break
        parts = zero
        for r, l, c in sweep(rows, comps, span):
            gain = alpha * field[r, l]
            solved[r, l] = gain if step == 0 else solved[r, l] + gain
            left = resid[r, l] - alpha * image[r, l]
            resid[r, l] = left
            parts = parts + fold(left * left)
        following = total(parts)
        beta = following / jnp.maximum(norm, 1.0)
        norm = following
        for r, l, c in sweep(rows, comps, span):
            d = resid[r, l] + beta * field[r, l]
            field[r, l] = d
            keep(r, c, d)
    for r, l, c in sweep(rows, comps, span):
        x = solved[r, l] + alpha * field[r, l]
        pushed = flow(c, r) * x
        image[r, 0:span] = pushed if c == 0 else image[r, 0:span] + pushed
        keep(r, c, (1.5 - weight[r, :]) * x)
    updated[...] = hist[...] + weight[...] * image[:, 0:span]
    sent = blocks[0]
    put(sent, 0, placed_rows(first, sent.shape[0], place, [*earlier_updated, updated]))
    out = s
    for c in range(comps):
        cpl = cstack[c].astype(jnp.bfloat16)
        main = dot(cpl, split[0:rows, c * span:(c + 1) * span])
        minor = dot(cpl, split[0:rows, wide + c * span:wide + (c + 1) * span])
        out = out + scale * (main[0:8] + main[16:24] + minor[0:8])
    stress[...] = out


def placed_rows(first, count, place, sources):
    width = sum(source.shape[1] for source in sources)
    placing = hot(place[0:1, 0:width] - first, count)
    sums, left = 0.0, 0
    for source in sources:
        hi, lo = halves(source[...])
        cut = placing[:, left:left + source.shape[1]]
        sums = sums + (dot(cut, hi, NT) + dot(cut, lo, NT))
        left += source.shape[1]
    return sums


def put(block, top, rows):
    height, filled = rows.shape
    block[pl.ds(top, height), 0:filled] = rows
    rest = jnp.zeros((height, block.shape[1] - filled), jnp.float32)
    block[pl.ds(top, height), filled:] = rest


def ship_kernel(devices, first, chunks, place, at, *refs):
    updated, stress, (pair, out) = refs[:chunks], refs[chunks:2 * chunks], refs[2 * chunks:]
    me, plane, lane, lanes = whereabouts(devices)
    group = pair.shape[0] // 2
    rows = placed_rows(first, 2 * group, place, updated)
    put(pair, pl.multiple_of((1 - plane // 2) * group, group), rows[0:group])
    put(pair, pl.multiple_of(plane // 2 * group, group), rows[group:])
    hi, lo = halves(jnp.concatenate([ref[...] for ref in stress], axis=1))
    serves = hot(at[0:1, :], hi.shape[1])
    out[...] = (dot(hi, serves) + dot(lo, serves))[0:out.shape[0], :]


def hold_kernel(own_core, sibling, held):
    held[0] = own_core[...]
    held[1] = sibling[...]


def join_kernel(cap, held, own_core, sibling, *blocks):
    for i, block in enumerate(blocks):
        rows = slice(i * cap, (i + 1) * cap)
        block[0:cap, :] = held[0, rows, :]
        block[cap:2 * cap, :] = held[1, rows, :]
        block[2 * cap:3 * cap, :] = own_core[rows, :]
        block[3 * cap:, :] = sibling[rows, :]


def land(tile, out, stage, sem, slot, at):
    nodes = out.shape[0]
    stage[slot] = jnp.transpose(tile)[0:nodes, :]
    columns = pl.multiple_of(at * LANES, LANES)
    copy = pltpu.make_async_copy(stage.at[slot], out.at[:, pl.ds(columns, LANES)], sem.at[slot])
    copy.start()
    return copy


def land_group(block, count, plane, out, stage, sem, slot):
    height = block.shape[0] // count
    copies = []
    for part in range(count):
        tile = block[part * height:(part + 1) * height, :]
        copies.append(land(tile, out, stage, sem, slot + part, plane * count + part))
    return copies


def land_kernel(devices, cap, pair, *refs):
    blocks, (out, stage, sem, gather) = refs[:-4], refs[-4:]
    me, plane, lane, lanes = whereabouts(devices)
    group = pair.shape[0] // 2
    copies = []
    for part in range(2):
        source = jnp.where(plane // 2 == part, plane, plane ^ 3)
        block = pair.at[part * group:(part + 1) * group, :]
        copies += land_group(block, 2, source, out, stage, sem, 2 * part)
    for i, apart in enumerate((2, 1)):
        for k in range(lanes):
            at = pl.multiple_of((lane ^ k) * cap, cap)
            top = (2 * i + k % 2) * cap
            gather[i, pl.ds(at, cap), :] = blocks[k // 2][top:top + cap, :]
        copies += land_group(gather.at[i], 2, plane ^ apart, out, stage, sem, 4 + 2 * i)
    for copy in copies:
        copy.wait()


def params(mib=24):
    return pltpu.CompilerParams(vmem_limit_bytes=mib * 2**20)


def shards(
    history, yield_flags, strain, qp_to_rve, new_owner, stiffness, pattern, coupling, plastic_dir
):
    devices = lax.axis_size(("macro", "pool"))
    nodes, columns = history.shape
    comps, voigt = coupling.shape[0], coupling.shape[1]
    per_peer = 2 * columns // devices
    rows = up(nodes, 32)
    deep = up(nodes, 256)
    f32, bf16, i32 = jnp.float32, jnp.bfloat16, jnp.int32
    vmem = pl.BlockSpec(memory_space=pltpu.VMEM)
    small_inputs = (coupling, plastic_dir, strain, new_owner.reshape(1, columns), qp_to_rve, pattern)
    small = pl.pallas_call(
        pack_kernel,
        out_shape=jax.ShapeDtypeStruct((up(PATTERN + pattern.size, 8), nodes), f32),
        in_specs=[vmem] * 5 + [pl.BlockSpec(memory_space=pltpu.SMEM)],
        out_specs=vmem,
        compiler_params=params(60),
    )(*small_inputs)
    inputs = (small, stiffness, history, yield_flags)
    khi, klo, hist_s, weight_s, strain_s, place_s, qp_s, cstack, pdir = pl.pallas_call(
        functools.partial(prep_kernel, devices, per_peer, comps, voigt),
        out_shape=(
            jax.ShapeDtypeStruct((rows, deep), bf16),
            jax.ShapeDtypeStruct((rows, deep), bf16),
            jax.ShapeDtypeStruct((rows, columns), f32),
            jax.ShapeDtypeStruct((rows, columns), f32),
            jax.ShapeDtypeStruct((8, columns), f32),
            jax.ShapeDtypeStruct((8, columns), i32),
            jax.ShapeDtypeStruct((8, columns), i32),
            jax.ShapeDtypeStruct((comps, 32, rows), f32),
            jax.ShapeDtypeStruct((comps, rows, LANES), f32),
        ),
        in_specs=[pl.BlockSpec(memory_space=pltpu.HBM)] * 4,
        out_specs=[vmem] * 9,
        scratch_shapes=[pltpu.VMEM((rows, deep), f32), pltpu.VMEM((8, columns), f32)]
        + [pltpu.VMEM(x.shape, x.dtype) for x in inputs]
        + [pltpu.SemaphoreType.DMA((4,))],
        compiler_params=params(46),
    )(*inputs)

    lanes = devices // PLANES
    group = lanes * per_peer
    block = lambda height: jax.ShapeDtypeStruct((height, deep), f32)
    whole = lambda shape: pl.BlockSpec(shape, lambda i: (0,) * len(shape))
    updated, stress_s, ready = [], [], []
    left = 0
    for span in (LANES,) * (columns // LANES):
        part = lambda height: pl.BlockSpec((height, span), lambda i, at=left // span: (0, at))
        wide = comps * span
        outs = [block(LANES)]
        done = pl.pallas_call(
            functools.partial(solve_kernel, 1.0 / math.sqrt(comps * nodes), left, len(updated)),
            grid=(1,),
            out_shape=(
                jax.ShapeDtypeStruct((rows, span), f32),
                jax.ShapeDtypeStruct((8, span), f32),
                *outs,
            ),
            in_specs=[whole((rows, deep)), whole((rows, deep)), part(rows), part(rows), part(8),
                      whole((comps, 32, rows)), whole((comps, rows, LANES)), whole((8, columns))]
            + [whole(u.shape) for u in updated],
            out_specs=[whole((rows, span)), whole((8, span))] + [whole(o.shape) for o in outs],
            scratch_shapes=[pltpu.VMEM((rows, wide), f32) for _ in range(4)]
            + [pltpu.VMEM((deep, 2 * wide), bf16)],
            compiler_params=params(),
            cost_estimate=pl.CostEstimate(
                flops=18 * rows * deep * wide, bytes_accessed=2**20, transcendentals=0
            ),
        )(khi, klo, hist_s, weight_s, strain_s, cstack, pdir, place_s, *updated)
        updated.append(done[0])
        stress_s.append(done[1])
        ready.extend(done[2:])
        left += span
    pair, stress_out = pl.pallas_call(
        functools.partial(ship_kernel, devices, 2 * group, len(updated)),
        out_shape=(block(2 * group), jax.ShapeDtypeStruct((voigt, columns), f32)),
        in_specs=[vmem] * (2 + 2 * len(updated)),
        out_specs=[vmem] * 2,
        compiler_params=params(),
        cost_estimate=pl.CostEstimate(
            flops=4 * rows * columns * columns, bytes_accessed=2**20, transcendentals=0
        ),
    )(place_s, qp_s, *updated, *stress_s)

    axes = ("macro", "pool")

    def hop(sent, mask):
        return lax.ppermute(sent, axes, [(s, s ^ mask) for s in range(devices)])

    planes = [list(range(z * lanes, (z + 1) * lanes)) for z in range(PLANES)]
    pair = lax.all_to_all(
        pair.reshape(2 * lanes, per_peer, deep), axes, split_axis=0, concat_axis=0, tiled=True,
        axis_index_groups=[planes[0] + planes[3], planes[1] + planes[2]],
    ).reshape(2 * group, deep)
    held = pl.pallas_call(
        hold_kernel,
        out_shape=jax.ShapeDtypeStruct((2, LANES, deep), f32),
        in_specs=[vmem] * 2,
        out_specs=vmem,
        compiler_params=params(),
        cost_estimate=pl.CostEstimate(flops=2**40, bytes_accessed=2**20, transcendentals=0),
    )(hop(ready[0], 2 * lanes), hop(ready[1], 2 * lanes + 1))
    own_core, sibling = hop(ready[2], lanes), hop(ready[3], lanes + 1)
    own_core, sibling, held = lax.optimization_barrier((own_core, sibling, held))
    half = lanes // 2
    joined = pl.pallas_call(
        functools.partial(join_kernel, per_peer),
        out_shape=(block(4 * per_peer),) * half,
        in_specs=[vmem] * 3,
        out_specs=[vmem] * half,
        compiler_params=params(),
    )(held, own_core, sibling)
    joined = [sent if i == 0 else hop(sent, 2 * i) for i, sent in enumerate(joined)]
    new_history = pl.pallas_call(
        functools.partial(land_kernel, devices, per_peer),
        out_shape=jax.ShapeDtypeStruct((nodes, devices * per_peer), f32),
        in_specs=[vmem] * (1 + half),
        out_specs=pl.BlockSpec(memory_space=pl.ANY),
        scratch_shapes=[pltpu.VMEM((8, nodes, LANES), f32), pltpu.SemaphoreType.DMA((8,)),
                        pltpu.VMEM((2, group, deep), f32)],
        compiler_params=params(),
    )(pair, *joined)
    return (new_history, stress_out)


def solution(mesh):
    return jax.shard_map(
        shards,
        mesh=mesh,
        in_specs=(
            P(None, ("macro", "pool")),
            P(None, ("macro", "pool")),
            P(None, ("macro", "pool")),
            P(("macro", "pool"), None),
            P(("macro", "pool"), None),
            P(),
            P(),
            P(),
            P(),
        ),
        out_specs=(P(None, ("macro", "pool")), P(None, ("macro", "pool"))),
        check_vma=False,
    )
```

profile of v0, /device:TPU:0, one launch (start us, length us, event | category | flops | bytes accessed | tf_op | source)
XLA Modules:
  0.0 120.5 jit_solution(12872183553150125871)
XLA Ops:
  0.6 1.7 %shard_map.104.refs_0_ = f32[120,729]{1,0:T(8,128)} custom-call(f32[3,6,729]{2,1,0:T(8,128)} %coupling.1, f32[3,729]{1,0:T(4,128)} %plastic.1, f32[6,512]{1,0:T(8,128)} %strain.1, s32[1,512]{1,0:T(1,128)} %bitcast.3, s32[1,512]{1,0:T(1,128)} %qp.1, s32[9,9]{1,0:T(8,128)} %pattern.1), custom_call_target="tpu_custom_call" | custom-call | tf_op jit(solution)/shard_map/pallas_call | solution.py:341
  2.4 1.0 copy-done
  3.3 4.7 %shard_map.105 = (bf16[736,768]{1,0:T(8,128)(2,1)S(1)}, bf16[736,768]{1,0:T(8,128)(2,1)S(1)}, f32[736,512]{1,0:T(8,128)S(1)}, f32[736,512]{1,0:T(8,128)S(1)}, f3...) custom-call(f32[120,729]{1,0:T(8,128)S(1)} %copy-done, ...), custom_call_target="tpu_custom_call" | custom-call | tf_op jit(solution)/shard_map/pallas_call | solution.py:349
  8.1 8.3 %shard_map.106 = (f32[736,128]{1,0:T(8,128)S(1)}, f32[8,128]{1,0:T(8,128)S(1)}, f32[128,768]{1,0:T(8,128)S(1)}) custom-call(bf16[736,768]{1,0:T(8,128)(2,1)S(1)} %get-tuple-element.34.khi, bf16[736,768]{1,0:T(8,128)(2,1)S(1)} %get-tuple-element.35.klo, f32[736,512]{1,0:T(8,128)S(1)} %get-tuple-element.36.hist, f32[736,512]{1,0:T(8,128)S(1)} %get-tuple-element.37.weight, ...), custom_call_target="tpu_custom_call" | custom-call | flops 3906994176 | bytes 1048576 | tf_op jit(solution)/shard_map/pallas_call | solution.py:380
  16.4 4.1 %collective-permute-start.2 = (f32[128,768]{1,0:T(8,128)S(1)}, f32[128,768]{1,0:T(8,128)S(1)}, u32[]{:S(2)}, u32[]{:S(2)}) collective-permute-start(f32[128,768]{1,0:T(8,128)S(1)} %get-tuple-element.52), channel_id=1, source_target_pairs={{0,16},{1,17},{2,18},{3,19},{4,20},{5,21},{6,22},{7,23},{8,24},{9,... | collective-permute-start | bytes 1179656 | tf_op jit(solution)/shard_map/ppermute | solution.py:417
  20.5 8.4 %shard_map.107 = (f32[736,128]{1,0:T(8,128)S(1)}, f32[8,128]{1,0:T(8,128)S(1)}, f32[128,768]{1,0:T(8,128)S(1)}) custom-call(bf16[736,768]{1,0:T(8,128)(2,1)S(1)} %get-tuple-element.34.khi, bf16[736,768]{1,0:T(8,128)(2,1)S(1)} %get-tuple-element.35.klo, f32[736,512]{1,0:T(8,128)S(1)} %get-tuple-element.36.hist, f32[736,512]{1,0:T(8,128)S(1)} %get-tuple-element.37.weight, ...), custom_call_target="tpu_custom_call" | custom-call | flops 3906994176 | bytes 1048576 | tf_op jit(solution)/shard_map/pallas_call | solution.py:380
  28.9 0.1 collective-permute-start.3
  29.0 9.5 %shard_map.108 = (f32[736,128]{1,0:T(8,128)S(1)}, f32[8,128]{1,0:T(8,128)S(1)}, f32[128,768]{1,0:T(8,128)}) custom-call(bf16[736,768]{1,0:T(8,128)(2,1)S(1)} %get-tuple-element.34.khi, bf16[736,768]{1,0:T(8,128)(2,1)S(1)} %get-tuple-element.35.klo, f32[736,512]{1,0:T(8,128)S(1)} %get-tuple-element.36.hist, f32[736,512]{1,0:T(8,128)S(1)} %get-tuple-element.37.weight, ...), custom_call_target="tpu_custom_call" | custom-call | flops 3906994176 | bytes 1048576 | tf_op jit(solution)/shard_map/pallas_call | solution.py:380
  38.5 9.7 %shard_map.109 = (f32[736,128]{1,0:T(8,128)S(1)}, f32[8,128]{1,0:T(8,128)S(1)}, f32[128,768]{1,0:T(8,128)}) custom-call(bf16[736,768]{1,0:T(8,128)(2,1)S(1)} %get-tuple-element.34.khi, bf16[736,768]{1,0:T(8,128)(2,1)S(1)} %get-tuple-element.35.klo, f32[736,512]{1,0:T(8,128)S(1)} %get-tuple-element.36.hist, f32[736,512]{1,0:T(8,128)S(1)} %get-tuple-element.37.weight, ...), custom_call_target="tpu_custom_call" | custom-call | flops 3906994176 | bytes 1048576 | tf_op jit(solution)/shard_map/pallas_call | solution.py:380
  48.1 3.1 %shard_map.110 = (f32[512,768]{1,0:T(8,128)}, f32[6,512]{1,0:T(8,128)}) custom-call(s32[8,512]{1,0:T(8,128)S(1)} %get-tuple-element.32.place, s32[8,512]{1,0:T(8,128)S(1)} %get-tuple-element.33.at, f32[736,128]{1,0:T(8,128)S(1)} %get-tuple-element.41.refs_0_, f32[736,128]{1,0:T(8,128)S(1)} %get-tuple-element.42.refs_1_, ...), custom_call_target="tpu_custom_call" | custom-call | flops 771751936 | bytes 1048576 | tf_op jit(solution)/shard_map/pallas_call | solution.py:403
  51.2 6.9 %all-to-all-start = ((f32[16,32,768]{2,1,0:T(8,128)}), f32[16,32,768]{2,1,0:T(8,128)}, u32[]{:S(2)}, u32[]{:S(2)}) async-start(f32[16,32,768]{2,1,0:T(8,128)} %bitcast.1), calls=%async_computation | async-start | bytes 3145728 | tf_op jit(solution)/shard_map/all_to_all | solution.py:420
  58.2 0.1 collective-permute-start
  58.3 1.6 %collective-permute-start.1 = (f32[128,768]{1,0:T(8,128)}, f32[128,768]{1,0:T(8,128)}, u32[]{:S(2)}, u32[]{:S(2)}) collective-permute-start(f32[128,768]{1,0:T(8,128)} %get-tuple-element.51), channel_id=1, source_target_pairs={{0,9},{1,8},{2,11},{3,10},{4,13},{5,12},{6,15},{7,14},{8,1},{9,0},... | collective-permute-start | bytes 1179656 | tf_op jit(solution)/shard_map/ppermute | solution.py:417
  59.9 0.0 collective-permute-done.2.own_core
  59.9 0.1 shard_map.111.held
  60.0 27.4 %collective-permute-done.own_core = f32[128,768]{1,0:T(8,128)} collective-permute-done((f32[128,768]{1,0:T(8,128)}, f32[128,768]{1,0:T(8,128)}, u32[]{:S(2)}, u32[]{:S(2)}) %collective-permute-start) | collective-permute-done | bytes 393248 | tf_op jit(solution)/shard_map/ppermute | solution.py:417
  87.4 7.1 %collective-permute-done.1.sibling = f32[128,768]{1,0:T(8,128)} collective-permute-done((f32[128,768]{1,0:T(8,128)}, f32[128,768]{1,0:T(8,128)}, u32[]{:S(2)}, u32[]{:S(2)}) %collective-permute-start.1) | collective-permute-done | bytes 393248 | tf_op jit(solution)/shard_map/ppermute | solution.py:417
  94.5 1.2 %shard_map.112 = (f32[128,768]{1,0:T(8,128)S(1)}, f32[128,768]{1,0:T(8,128)S(1)}, f32[128,768]{1,0:T(8,128)S(1)}, f32[128,768]{1,0:T(8,128)S(1)}) custom-call(f32[2,128,768]{2,1,0:T(8,128)S(1)} %shard_map.111.held, f32[128,768]{1,0:T(8,128)} %collective-permute-done.own_core, f32[128,768]{1,0:T(8,128)} %collective-permute-done.1.sibling), custom_call_target="tpu_custom_call" | custom-call | tf_op jit(solution)/shard_map/pallas_call | solution.py:435
  95.7 1.6 %collective-permute-start.4 = (f32[128,768]{1,0:T(8,128)S(1)}, f32[128,768]{1,0:T(8,128)S(1)}, u32[]{:S(2)}, u32[]{:S(2)}) collective-permute-start(f32[128,768]{1,0:T(8,128)S(1)} %get-tuple-element.58), channel_id=1, source_target_pairs={{0,2},{1,3},{2,0},{3,1},{4,6},{5,7},{6,4},{7,5},{8,10},{9,11},{10,... | collective-permute-start | bytes 1179656 | tf_op jit(solution)/shard_map/ppermute | solution.py:417
  97.3 1.5 %collective-permute-start.5 = (f32[128,768]{1,0:T(8,128)S(1)}, f32[128,768]{1,0:T(8,128)S(1)}, u32[]{:S(2)}, u32[]{:S(2)}) collective-permute-start(f32[128,768]{1,0:T(8,128)S(1)} %get-tuple-element.59), channel_id=1, source_target_pairs={{0,4},{1,5},{2,6},{3,7},{4,0},{5,1},{6,2},{7,3},{8,12},{9,13},{10,... | collective-permute-start | bytes 1179656 | tf_op jit(solution)/shard_map/ppermute | solution.py:417
  98.8 0.5 collective-permute-start.6
  99.3 8.4 %collective-permute-done.4.refs_1_ = f32[128,768]{1,0:T(8,128)S(1)} collective-permute-done((f32[128,768]{1,0:T(8,128)S(1)}, f32[128,768]{1,0:T(8,128)S(1)}, u32[]{:S(2)}, u32[]{:S(2)}) %collective-permute-start.4) | collective-permute-done | bytes 393248 | tf_op jit(solution)/shard_map/ppermute | solution.py:417
  107.7 9.4 %collective-permute-done.5.refs_2_ = f32[128,768]{1,0:T(8,128)S(1)} collective-permute-done((f32[128,768]{1,0:T(8,128)S(1)}, f32[128,768]{1,0:T(8,128)S(1)}, u32[]{:S(2)}, u32[]{:S(2)}) %collective-permute-start.5) | collective-permute-done | bytes 393248 | tf_op jit(solution)/shard_map/ppermute | solution.py:417
  117.1 3.3 %shard_map.113 = f32[729,1024]{1,0:T(8,128)} custom-call(f32[512,768]{1,0:T(8,128)} %bitcast.2.pair, f32[128,768]{1,0:T(8,128)S(1)} %get-tuple-element.57.refs_0_, f32[128,768]{1,0:T(8,128)S(1)} %collective-permute-done.4.refs_1_, f32[128,768]{1,0:T(8,128)S(1)} %collective-permute-done.5.refs_2_, f32[128,768]{1,0:T(8,128)S(1)} %collective-permute-done.6.refs_3_), custom_call_target="tpu_custom_call" | custom-call | tf_op jit(solution)/shard_map/pallas_call | solution.py:443
  (4 shorter events, 0.0 us)
Async XLA Ops:
  2.4 1.0 copy-start
  16.4 43.5 %collective-permute-start.2 = (f32[128,768]{1,0:T(8,128)S(1)}, f32[128,768]{1,0:T(8,128)S(1)}, u32[]{:S(2)}, u32[]{:S(2)}) collective-permute-start(f32[128,768]{1,0:T(8,128)S(1)} %get-tuple-element.52), channel_id=1, source_target_pairs={{0,16},{1,17},{2,18},{3,19},{4,20},{5,21},{6,22},{7,23},{8,24},{9,... | collective-permute-start | bytes 1179656 | tf_op jit(solution)/shard_map/ppermute | solution.py:417
  28.9 31.0 %collective-permute-start.3 = (f32[128,768]{1,0:T(8,128)S(1)}, f32[128,768]{1,0:T(8,128)S(1)}, u32[]{:S(2)}, u32[]{:S(2)}) collective-permute-start(f32[128,768]{1,0:T(8,128)S(1)} %get-tuple-element.53), channel_id=1, source_target_pairs={{0,17},{1,16},{2,19},{3,18},{4,21},{5,20},{6,23},{7,22},{8,25},{9,... | collective-permute-start | bytes 1179656 | tf_op jit(solution)/shard_map/ppermute | solution.py:417
  51.2 65.9 %all-to-all-start = ((f32[16,32,768]{2,1,0:T(8,128)}), f32[16,32,768]{2,1,0:T(8,128)}, u32[]{:S(2)}, u32[]{:S(2)}) async-start(f32[16,32,768]{2,1,0:T(8,128)} %bitcast.1), calls=%async_computation | async-start | bytes 3145728 | tf_op jit(solution)/shard_map/all_to_all | solution.py:420
  58.2 29.2 %collective-permute-start = (f32[128,768]{1,0:T(8,128)}, f32[128,768]{1,0:T(8,128)}, u32[]{:S(2)}, u32[]{:S(2)}) collective-permute-start(f32[128,768]{1,0:T(8,128)} %get-tuple-element.50), channel_id=1, source_target_pairs={{0,8},{1,9},{2,10},{3,11},{4,12},{5,13},{6,14},{7,15},{8,0},{9,1},... | collective-permute-start | bytes 1179656 | tf_op jit(solution)/shard_map/ppermute | solution.py:417
  58.3 36.3 %collective-permute-start.1 = (f32[128,768]{1,0:T(8,128)}, f32[128,768]{1,0:T(8,128)}, u32[]{:S(2)}, u32[]{:S(2)}) collective-permute-start(f32[128,768]{1,0:T(8,128)} %get-tuple-element.51), channel_id=1, source_target_pairs={{0,9},{1,8},{2,11},{3,10},{4,13},{5,12},{6,15},{7,14},{8,1},{9,0},... | collective-permute-start | bytes 1179656 | tf_op jit(solution)/shard_map/ppermute | solution.py:417
  95.7 12.0 %collective-permute-start.4 = (f32[128,768]{1,0:T(8,128)S(1)}, f32[128,768]{1,0:T(8,128)S(1)}, u32[]{:S(2)}, u32[]{:S(2)}) collective-permute-start(f32[128,768]{1,0:T(8,128)S(1)} %get-tuple-element.58), channel_id=1, source_target_pairs={{0,2},{1,3},{2,0},{3,1},{4,6},{5,7},{6,4},{7,5},{8,10},{9,11},{10,... | collective-permute-start | bytes 1179656 | tf_op jit(solution)/shard_map/ppermute | solution.py:417
  97.3 19.8 %collective-permute-start.5 = (f32[128,768]{1,0:T(8,128)S(1)}, f32[128,768]{1,0:T(8,128)S(1)}, u32[]{:S(2)}, u32[]{:S(2)}) collective-permute-start(f32[128,768]{1,0:T(8,128)S(1)} %get-tuple-element.59), channel_id=1, source_target_pairs={{0,4},{1,5},{2,6},{3,7},{4,0},{5,1},{6,2},{7,3},{8,12},{9,13},{10,... | collective-permute-start | bytes 1179656 | tf_op jit(solution)/shard_map/ppermute | solution.py:417
  98.8 18.3 %collective-permute-start.6 = (f32[128,768]{1,0:T(8,128)S(1)}, f32[128,768]{1,0:T(8,128)S(1)}, u32[]{:S(2)}, u32[]{:S(2)}) collective-permute-start(f32[128,768]{1,0:T(8,128)S(1)} %get-tuple-element.60), channel_id=1, source_target_pairs={{0,6},{1,7},{2,4},{3,5},{4,2},{5,3},{6,0},{7,1},{8,14},{9,15},{10,... | collective-permute-start | bytes 1179656 | tf_op jit(solution)/shard_map/ppermute | solution.py:417
where the time goes:
time: 121 us
  waiting for transfers between devices  52.4 us (43%)
  Pallas kernels  50 us (41%)
  starting transfers between devices  16.4 us (14%)
    ppermute x7, waiting for transfers between devices, hop(): return lax.ppermute(sent, axes, [(s, s ^ mask) for s in range(devices)])  52.4 us
    pallas_call x4, Pallas kernels, shards(): pl.pallas_call(functools.partial(solve_kernel, 1.0 / math.sqrt(comps * no...  35.9 us
    ppermute x7, starting transfers between devices, hop(): return lax.ppermute(sent, axes, [(s, s ^ mask) for s in range(devices)])  9.43 us
    all_to_all x1, starting transfers between devices, shards(): lax.all_to_all(pair.reshape(2 * lanes, per_peer, deep), axes, split_axis=...  6.94 us
    pallas_call x1, Pallas kernels, shards(): pl.pallas_call(functools.partial(prep_kernel, devices, per_peer, comps, v...  4.72 us
    pallas_call x1, Pallas kernels, shards(): pl.pallas_call(functools.partial(land_kernel, devices, per_peer), out_sha...  3.27 us
    pallas_call x1, Pallas kernels, shards(): pl.pallas_call(functools.partial(ship_kernel, devices, 2 * group, len(upd...  3.09 us
  transfers between devices with their start and end apart: 8, of which 4 were waited for; matrix products, arithmetic and copies ran while one was open for 0% of the time, Pallas kernels for 26%

commit v1 on v0

--- a/solution.py
+++ b/solution.py
@@ -271,18 +271,11 @@
     out[...] = (dot(hi, serves) + dot(lo, serves))[0:out.shape[0], :]
 
 
-def hold_kernel(own_core, sibling, held):
-    held[0] = own_core[...]
-    held[1] = sibling[...]
-
-
-def join_kernel(cap, held, own_core, sibling, *blocks):
+def join_kernel(cap, *refs):
+    landed, blocks = refs[:4], refs[4:]
     for i, block in enumerate(blocks):
-        rows = slice(i * cap, (i + 1) * cap)
-        block[0:cap, :] = held[0, rows, :]
-        block[cap:2 * cap, :] = held[1, rows, :]
-        block[2 * cap:3 * cap, :] = own_core[rows, :]
-        block[3 * cap:, :] = sibling[rows, :]
+        for k, rows in enumerate(landed):
+            block[k * cap:(k + 1) * cap, :] = rows[i * cap:(i + 1) * cap, :]
 
 
 def land(tile, out, stage, sem, slot, at):
@@ -421,24 +414,20 @@
         pair.reshape(2 * lanes, per_peer, deep), axes, split_axis=0, concat_axis=0, tiled=True,
         axis_index_groups=[planes[0] + planes[3], planes[1] + planes[2]],
     ).reshape(2 * group, deep)
-    held = pl.pallas_call(
-        hold_kernel,
-        out_shape=jax.ShapeDtypeStruct((2, LANES, deep), f32),
-        in_specs=[vmem] * 2,
-        out_specs=vmem,
-        compiler_params=params(),
-        cost_estimate=pl.CostEstimate(flops=2**40, bytes_accessed=2**20, transcendentals=0),
-    )(hop(ready[0], 2 * lanes), hop(ready[1], 2 * lanes + 1))
-    own_core, sibling = hop(ready[2], lanes), hop(ready[3], lanes + 1)
-    own_core, sibling, held = lax.optimization_barrier((own_core, sibling, held))
+    hops = (2 * lanes, 2 * lanes + 1, lanes, lanes + 1)
+    landed = []
+    for sent, mask in zip(ready, hops):
+        landed.append(hop(sent, mask))
+        landed[-2:] = lax.optimization_barrier(tuple(landed[-2:]))
     half = lanes // 2
     joined = pl.pallas_call(
         functools.partial(join_kernel, per_peer),
         out_shape=(block(4 * per_peer),) * half,
-        in_specs=[vmem] * 3,
+        in_specs=[vmem] * 4,
         out_specs=[vmem] * half,
         compiler_params=params(),
-    )(held, own_core, sibling)
+        cost_estimate=pl.CostEstimate(flops=2**40, bytes_accessed=2**20, transcendentals=0),
+    )(*landed)
     joined = [sent if i == 0 else hop(sent, 2 * i) for i, sent in enumerate(joined)]
     new_history = pl.pallas_call(
         functools.partial(land_kernel, devices, per_peer),

time: 121 us -> 113 us (0.934)
  waiting for transfers between devices: 52.4 us -> 45.7 us
  Pallas kernels: 50 us -> 47.3 us
    ppermute x7, waiting for transfers between devices: 52.4 us -> 45.7 us  [hop(): return lax.ppermute(sent, axes, [(s, s ^ mask) for s in range(devices)])]
    pallas_call x4, Pallas kernels: 35.9 us -> 34.4 us  [shards(): pl.pallas_call(functools.partial(solve_kernel, 1.0 / math.sqrt(comps * no...]
where the time goes in v1:
time: 113 us; the launch traced here: 111 us
  Pallas kernels  47.3 us (42%)
  waiting for transfers between devices  45.7 us (40%)
  starting transfers between devices  16.5 us (15%)
    ppermute x7, waiting for transfers between devices, hop(): return lax.ppermute(sent, axes, [(s, s ^ mask) for s in range(devices)])  45.7 us
    pallas_call x4, Pallas kernels, shards(): pl.pallas_call(functools.partial(solve_kernel, 1.0 / math.sqrt(comps * no...  34.4 us
    ppermute x7, starting transfers between devices, hop(): return lax.ppermute(sent, axes, [(s, s ^ mask) for s in range(devices)])  9.47 us
    all_to_all x1, starting transfers between devices, shards(): lax.all_to_all(pair.reshape(2 * lanes, per_peer, deep), axes, split_axis=...  7.06 us
    pallas_call x1, Pallas kernels, shards(): pl.pallas_call(functools.partial(prep_kernel, devices, per_peer, comps, v...  4.72 us
    pallas_call x1, Pallas kernels, shards(): pl.pallas_call(functools.partial(land_kernel, devices, per_peer), out_sha...  3.27 us
    pallas_call x1, Pallas kernels, shards(): pl.pallas_call(functools.partial(ship_kernel, devices, 2 * group, len(upd...  3.09 us
  transfers between devices with their start and end apart: 8, of which 4 were waited for; matrix products, arithmetic and copies ran while one was open for 0% of the time, Pallas kernels for 26%

profile of v1, /device:TPU:0, one launch (start us, length us, event | category | flops | bytes accessed | tf_op | source)
XLA Modules:
  0.0 111.4 jit_solution(17475044148989312161)
XLA Ops:
  0.6 1.7 %shard_map.104.refs_0_ = f32[120,729]{1,0:T(8,128)} custom-call(f32[3,6,729]{2,1,0:T(8,128)} %coupling.1, f32[3,729]{1,0:T(4,128)} %plastic.1, f32[6,512]{1,0:T(8,128)} %strain.1, s32[1,512]{1,0:T(1,128)} %bitcast.3, s32[1,512]{1,0:T(1,128)} %qp.1, s32[9,9]{1,0:T(8,128)} %pattern.1), custom_call_target="tpu_custom_call" | custom-call | tf_op jit(solution)/shard_map/pallas_call | solution.py:334
  2.4 1.0 copy-done
  3.3 4.7 %shard_map.105 = (bf16[736,768]{1,0:T(8,128)(2,1)S(1)}, bf16[736,768]{1,0:T(8,128)(2,1)S(1)}, f32[736,512]{1,0:T(8,128)S(1)}, f32[736,512]{1,0:T(8,128)S(1)}, f3...) custom-call(f32[120,729]{1,0:T(8,128)S(1)} %copy-done, ...), custom_call_target="tpu_custom_call" | custom-call | tf_op jit(solution)/shard_map/pallas_call | solution.py:342
  8.1 8.3 %shard_map.106 = (f32[736,128]{1,0:T(8,128)S(1)}, f32[8,128]{1,0:T(8,128)S(1)}, f32[128,768]{1,0:T(8,128)S(1)}) custom-call(bf16[736,768]{1,0:T(8,128)(2,1)S(1)} %get-tuple-element.37.khi, bf16[736,768]{1,0:T(8,128)(2,1)S(1)} %get-tuple-element.38.klo, f32[736,512]{1,0:T(8,128)S(1)} %get-tuple-element.39.hist, f32[736,512]{1,0:T(8,128)S(1)} %get-tuple-element.40.weight, ...), custom_call_target="tpu_custom_call" | custom-call | flops 3906994176 | bytes 1048576 | tf_op jit(solution)/shard_map/pallas_call | solution.py:373
  16.4 4.1 %collective-permute-start = (f32[128,768]{1,0:T(8,128)S(1)}, f32[128,768]{1,0:T(8,128)S(1)}, u32[]{:S(2)}, u32[]{:S(2)}) collective-permute-start(f32[128,768]{1,0:T(8,128)S(1)} %get-tuple-element.53), channel_id=1, source_target_pairs={{0,16},{1,17},{2,18},{3,19},{4,20},{5,21},{6,22},{7,23},{8,24},{9,... | collective-permute-start | bytes 1179656 | tf_op jit(solution)/shard_map/ppermute | solution.py:410
  20.5 8.4 %shard_map.107 = (f32[736,128]{1,0:T(8,128)S(1)}, f32[8,128]{1,0:T(8,128)S(1)}, f32[128,768]{1,0:T(8,128)S(1)}) custom-call(bf16[736,768]{1,0:T(8,128)(2,1)S(1)} %get-tuple-element.37.khi, bf16[736,768]{1,0:T(8,128)(2,1)S(1)} %get-tuple-element.38.klo, f32[736,512]{1,0:T(8,128)S(1)} %get-tuple-element.39.hist, f32[736,512]{1,0:T(8,128)S(1)} %get-tuple-element.40.weight, ...), custom_call_target="tpu_custom_call" | custom-call | flops 3906994176 | bytes 1048576 | tf_op jit(solution)/shard_map/pallas_call | solution.py:373
  28.9 0.1 collective-permute-start.1
  29.0 8.7 %shard_map.108 = (f32[736,128]{1,0:T(8,128)S(1)}, f32[8,128]{1,0:T(8,128)S(1)}, f32[128,768]{1,0:T(8,128)S(1)}) custom-call(bf16[736,768]{1,0:T(8,128)(2,1)S(1)} %get-tuple-element.37.khi, bf16[736,768]{1,0:T(8,128)(2,1)S(1)} %get-tuple-element.38.klo, f32[736,512]{1,0:T(8,128)S(1)} %get-tuple-element.39.hist, f32[736,512]{1,0:T(8,128)S(1)} %get-tuple-element.40.weight, ...), custom_call_target="tpu_custom_call" | custom-call | flops 3906994176 | bytes 1048576 | tf_op jit(solution)/shard_map/pallas_call | solution.py:373
  37.7 1.6 %collective-permute-start.2 = (f32[128,768]{1,0:T(8,128)S(1)}, f32[128,768]{1,0:T(8,128)S(1)}, u32[]{:S(2)}, u32[]{:S(2)}) collective-permute-start(f32[128,768]{1,0:T(8,128)S(1)} %get-tuple-element.57), channel_id=1, source_target_pairs={{0,8},{1,9},{2,10},{3,11},{4,12},{5,13},{6,14},{7,15},{8,0},{9,1},... | collective-permute-start | bytes 1179656 | tf_op jit(solution)/shard_map/ppermute | solution.py:410
  39.3 8.9 %shard_map.109 = (f32[736,128]{1,0:T(8,128)S(1)}, f32[8,128]{1,0:T(8,128)S(1)}, f32[128,768]{1,0:T(8,128)S(1)}) custom-call(bf16[736,768]{1,0:T(8,128)(2,1)S(1)} %get-tuple-element.37.khi, bf16[736,768]{1,0:T(8,128)(2,1)S(1)} %get-tuple-element.38.klo, f32[736,512]{1,0:T(8,128)S(1)} %get-tuple-element.39.hist, f32[736,512]{1,0:T(8,128)S(1)} %get-tuple-element.40.weight, ...), custom_call_target="tpu_custom_call" | custom-call | flops 3906994176 | bytes 1048576 | tf_op jit(solution)/shard_map/pallas_call | solution.py:373
  48.3 0.1 collective-permute-start.3
  48.4 3.1 %shard_map.110 = (f32[512,768]{1,0:T(8,128)}, f32[6,512]{1,0:T(8,128)}) custom-call(s32[8,512]{1,0:T(8,128)S(1)} %get-tuple-element.35.place, s32[8,512]{1,0:T(8,128)S(1)} %get-tuple-element.36.at, f32[736,128]{1,0:T(8,128)S(1)} %get-tuple-element.44.refs_0_, f32[736,128]{1,0:T(8,128)S(1)} %get-tuple-element.45.refs_1_, ...), custom_call_target="tpu_custom_call" | custom-call | flops 771751936 | bytes 1048576 | tf_op jit(solution)/shard_map/pallas_call | solution.py:396
  51.5 7.1 %all-to-all-start = ((f32[16,32,768]{2,1,0:T(8,128)}), f32[16,32,768]{2,1,0:T(8,128)}, u32[]{:S(2)}, u32[]{:S(2)}) async-start(f32[16,32,768]{2,1,0:T(8,128)} %bitcast.1), calls=%async_computation | async-start | bytes 3145728 | tf_op jit(solution)/shard_map/all_to_all | solution.py:413
  58.5 0.0 collective-permute-done.refs_0_
  58.6 3.9 %collective-permute-done.2.refs_2_ = f32[128,768]{1,0:T(8,128)S(1)} collective-permute-done((f32[128,768]{1,0:T(8,128)S(1)}, f32[128,768]{1,0:T(8,128)S(1)}, u32[]{:S(2)}, u32[]{:S(2)}) %collective-permute-start.2) | collective-permute-done | bytes 393248 | tf_op jit(solution)/shard_map/ppermute | solution.py:410
  62.5 24.0 %collective-permute-done.3.refs_3_ = f32[128,768]{1,0:T(8,128)S(1)} collective-permute-done((f32[128,768]{1,0:T(8,128)S(1)}, f32[128,768]{1,0:T(8,128)S(1)}, u32[]{:S(2)}, u32[]{:S(2)}) %collective-permute-start.3) | collective-permute-done | bytes 393248 | tf_op jit(solution)/shard_map/ppermute | solution.py:410
  86.4 0.1 shard_map.111
  86.5 2.0 %collective-permute-start.4 = (f32[128,768]{1,0:T(8,128)S(1)}, f32[128,768]{1,0:T(8,128)S(1)}, u32[]{:S(2)}, u32[]{:S(2)}) collective-permute-start(f32[128,768]{1,0:T(8,128)S(1)} %get-tuple-element.64), channel_id=1, source_target_pairs={{0,2},{1,3},{2,0},{3,1},{4,6},{5,7},{6,4},{7,5},{8,10},{9,11},{10,... | collective-permute-start | bytes 1179656 | tf_op jit(solution)/shard_map/ppermute | solution.py:410
  88.5 1.5 %collective-permute-start.5 = (f32[128,768]{1,0:T(8,128)S(1)}, f32[128,768]{1,0:T(8,128)S(1)}, u32[]{:S(2)}, u32[]{:S(2)}) collective-permute-start(f32[128,768]{1,0:T(8,128)S(1)} %get-tuple-element.65), channel_id=1, source_target_pairs={{0,4},{1,5},{2,6},{3,7},{4,0},{5,1},{6,2},{7,3},{8,12},{9,13},{10,... | collective-permute-start | bytes 1179656 | tf_op jit(solution)/shard_map/ppermute | solution.py:410
  90.0 0.0 collective-permute-start.6
  90.1 8.4 %collective-permute-done.4.refs_1_ = f32[128,768]{1,0:T(8,128)S(1)} collective-permute-done((f32[128,768]{1,0:T(8,128)S(1)}, f32[128,768]{1,0:T(8,128)S(1)}, u32[]{:S(2)}, u32[]{:S(2)}) %collective-permute-start.4) | collective-permute-done | bytes 393248 | tf_op jit(solution)/shard_map/ppermute | solution.py:410
  98.5 9.5 %collective-permute-done.5.refs_2_ = f32[128,768]{1,0:T(8,128)S(1)} collective-permute-done((f32[128,768]{1,0:T(8,128)S(1)}, f32[128,768]{1,0:T(8,128)S(1)}, u32[]{:S(2)}, u32[]{:S(2)}) %collective-permute-start.5) | collective-permute-done | bytes 393248 | tf_op jit(solution)/shard_map/ppermute | solution.py:410
  108.0 0.0 collective-permute-done.6.refs_3_
  108.0 3.3 %shard_map.112 = f32[729,1024]{1,0:T(8,128)} custom-call(f32[512,768]{1,0:T(8,128)} %bitcast.2.pair, f32[128,768]{1,0:T(8,128)S(1)} %get-tuple-element.63.refs_0_, f32[128,768]{1,0:T(8,128)S(1)} %collective-permute-done.4.refs_1_, f32[128,768]{1,0:T(8,128)S(1)} %collective-permute-done.5.refs_2_, f32[128,768]{1,0:T(8,128)S(1)} %collective-permute-done.6.refs_3_), custom_call_target="tpu_custom_call" | custom-call | tf_op jit(solution)/shard_map/pallas_call | solution.py:432
  (3 shorter events, 0.0 us)
Async XLA Ops:
  2.4 1.0 copy-start
  16.4 42.1 %collective-permute-start = (f32[128,768]{1,0:T(8,128)S(1)}, f32[128,768]{1,0:T(8,128)S(1)}, u32[]{:S(2)}, u32[]{:S(2)}) collective-permute-start(f32[128,768]{1,0:T(8,128)S(1)} %get-tuple-element.53), channel_id=1, source_target_pairs={{0,16},{1,17},{2,18},{3,19},{4,20},{5,21},{6,22},{7,23},{8,24},{9,... | collective-permute-start | bytes 1179656 | tf_op jit(solution)/shard_map/ppermute | solution.py:410
  28.9 29.6 %collective-permute-start.1 = (f32[128,768]{1,0:T(8,128)S(1)}, f32[128,768]{1,0:T(8,128)S(1)}, u32[]{:S(2)}, u32[]{:S(2)}) collective-permute-start(f32[128,768]{1,0:T(8,128)S(1)} %get-tuple-element.54), channel_id=1, source_target_pairs={{0,17},{1,16},{2,19},{3,18},{4,21},{5,20},{6,23},{7,22},{8,25},{9,... | collective-permute-start | bytes 1179656 | tf_op jit(solution)/shard_map/ppermute | solution.py:410
  37.7 24.8 %collective-permute-start.2 = (f32[128,768]{1,0:T(8,128)S(1)}, f32[128,768]{1,0:T(8,128)S(1)}, u32[]{:S(2)}, u32[]{:S(2)}) collective-permute-start(f32[128,768]{1,0:T(8,128)S(1)} %get-tuple-element.57), channel_id=1, source_target_pairs={{0,8},{1,9},{2,10},{3,11},{4,12},{5,13},{6,14},{7,15},{8,0},{9,1},... | collective-permute-start | bytes 1179656 | tf_op jit(solution)/shard_map/ppermute | solution.py:410
  48.3 38.2 %collective-permute-start.3 = (f32[128,768]{1,0:T(8,128)S(1)}, f32[128,768]{1,0:T(8,128)S(1)}, u32[]{:S(2)}, u32[]{:S(2)}) collective-permute-start(f32[128,768]{1,0:T(8,128)S(1)} %get-tuple-element.60), channel_id=1, source_target_pairs={{0,9},{1,8},{2,11},{3,10},{4,13},{5,12},{6,15},{7,14},{8,1},{9,0},... | collective-permute-start | bytes 1179656 | tf_op jit(solution)/shard_map/ppermute | solution.py:410
  51.5 56.5 %all-to-all-start = ((f32[16,32,768]{2,1,0:T(8,128)}), f32[16,32,768]{2,1,0:T(8,128)}, u32[]{:S(2)}, u32[]{:S(2)}) async-start(f32[16,32,768]{2,1,0:T(8,128)} %bitcast.1), calls=%async_computation | async-start | bytes 3145728 | tf_op jit(solution)/shard_map/all_to_all | solution.py:413
  86.5 12.0 %collective-permute-start.4 = (f32[128,768]{1,0:T(8,128)S(1)}, f32[128,768]{1,0:T(8,128)S(1)}, u32[]{:S(2)}, u32[]{:S(2)}) collective-permute-start(f32[128,768]{1,0:T(8,128)S(1)} %get-tuple-element.64), channel_id=1, source_target_pairs={{0,2},{1,3},{2,0},{3,1},{4,6},{5,7},{6,4},{7,5},{8,10},{9,11},{10,... | collective-permute-start | bytes 1179656 | tf_op jit(solution)/shard_map/ppermute | solution.py:410
  88.5 19.4 %collective-permute-start.5 = (f32[128,768]{1,0:T(8,128)S(1)}, f32[128,768]{1,0:T(8,128)S(1)}, u32[]{:S(2)}, u32[]{:S(2)}) collective-permute-start(f32[128,768]{1,0:T(8,128)S(1)} %get-tuple-element.65), channel_id=1, source_target_pairs={{0,4},{1,5},{2,6},{3,7},{4,0},{5,1},{6,2},{7,3},{8,12},{9,13},{10,... | collective-permute-start | bytes 1179656 | tf_op jit(solution)/shard_map/ppermute | solution.py:410
  90.0 17.9 %collective-permute-start.6 = (f32[128,768]{1,0:T(8,128)S(1)}, f32[128,768]{1,0:T(8,128)S(1)}, u32[]{:S(2)}, u32[]{:S(2)}) collective-permute-start(f32[128,768]{1,0:T(8,128)S(1)} %get-tuple-element.66), channel_id=1, source_target_pairs={{0,6},{1,7},{2,4},{3,5},{4,2},{5,3},{6,0},{7,1},{8,14},{9,15},{10,... | collective-permute-start | bytes 1179656 | tf_op jit(solution)/shard_map/ppermute | solution.py:410

commit v2 on v1

--- a/solution.py
+++ b/solution.py
@@ -80,9 +80,9 @@
     apart = owner // lanes ^ plane
     target = owner % lanes
     away = target ^ lane
-    shifted = away % 2 * (lanes // 2) + away // 2
-    turn = jnp.where(apart == 2, 0, jnp.where(apart == 1, 1, jnp.where(apart == 3, 2, 3)))
-    key = turn * lanes + jnp.where((apart == 2) | (apart == 1), shifted, target)
+    hopping = (away % 2 * 2 + jnp.where(apart == 2, 0, 1)) * (lanes // 2) + away // 2
+    staying = jnp.where(apart == 3, 2, 3) * lanes + target
+    key = jnp.where((apart == 2) | (apart == 1), hopping, staying)
     key_ids = lax.broadcasted_iota(jnp.int32, (devices, columns), 0)
     mine = jnp.where(key_ids == key, 1.0, 0.0)
     earlier = jnp.where(
@@ -308,7 +308,7 @@
     for i, apart in enumerate((2, 1)):
         for k in range(lanes):
             at = pl.multiple_of((lane ^ k) * cap, cap)
-            top = (2 * i + k % 2) * cap
+            top = (2 * (k % 2) + i) * cap
             gather[i, pl.ds(at, cap), :] = blocks[k // 2][top:top + cap, :]
         copies += land_group(gather.at[i], 2, plane ^ apart, out, stage, sem, 4 + 2 * i)
     for copy in copies:
@@ -414,7 +414,7 @@
         pair.reshape(2 * lanes, per_peer, deep), axes, split_axis=0, concat_axis=0, tiled=True,
         axis_index_groups=[planes[0] + planes[3], planes[1] + planes[2]],
     ).reshape(2 * group, deep)
-    hops = (2 * lanes, 2 * lanes + 1, lanes, lanes + 1)
+    hops = (2 * lanes, lanes, 2 * lanes + 1, lanes + 1)
     landed = []
     for sent, mask in zip(ready, hops):
         landed.append(hop(sent, mask))

time: 113 us -> 111 us (0.982)
  waiting for transfers between devices: 45.7 us -> 43.1 us
    ppermute x7, waiting for transfers between devices: 45.7 us -> 43.1 us  [hop(): return lax.ppermute(sent, axes, [(s, s ^ mask) for s in range(devices)])]
  transfers between devices with their start and end apart: 8 -> 8, of which waited for: 4 -> 4; matrix products, arithmetic and copies ran while one was open for 0% -> 0% of each run, Pallas kernels for 26% -> 27%
where the time goes in v2:
time: 111 us; the launch traced here: 109 us
  Pallas kernels  47.3 us (43%)
  waiting for transfers between devices  43.1 us (39%)
  starting transfers between devices  16.8 us (15%)
    ppermute x7, waiting for transfers between devices, hop(): return lax.ppermute(sent, axes, [(s, s ^ mask) for s in range(devices)])  43.1 us
    pallas_call x4, Pallas kernels, shards(): pl.pallas_call(functools.partial(solve_kernel, 1.0 / math.sqrt(comps * no...  34.4 us
    ppermute x7, starting transfers between devices, hop(): return lax.ppermute(sent, axes, [(s, s ^ mask) for s in range(devices)])  9.59 us
    all_to_all x1, starting transfers between devices, shards(): lax.all_to_all(pair.reshape(2 * lanes, per_peer, deep), axes, split_axis=...  7.23 us
    pallas_call x1, Pallas kernels, shards(): pl.pallas_call(functools.partial(prep_kernel, devices, per_peer, comps, v...  4.72 us
    pallas_call x1, Pallas kernels, shards(): pl.pallas_call(functools.partial(land_kernel, devices, per_peer), out_sha...  3.27 us
    pallas_call x1, Pallas kernels, shards(): pl.pallas_call(functools.partial(ship_kernel, devices, 2 * group, len(upd...  3.09 us
  transfers between devices with their start and end apart: 8, of which 4 were waited for; matrix products, arithmetic and copies ran while one was open for 0% of the time, Pallas kernels for 27%

profile of v2, /device:TPU:0, one launch (start us, length us, event | category | flops | bytes accessed | tf_op | source)
XLA Modules:
  0.0 109.0 jit_solution(6203240000536138170)
XLA Ops:
  0.6 1.7 %shard_map.104.refs_0_ = f32[120,729]{1,0:T(8,128)} custom-call(f32[3,6,729]{2,1,0:T(8,128)} %coupling.1, f32[3,729]{1,0:T(4,128)} %plastic.1, f32[6,512]{1,0:T(8,128)} %strain.1, s32[1,512]{1,0:T(1,128)} %bitcast.3, s32[1,512]{1,0:T(1,128)} %qp.1, s32[9,9]{1,0:T(8,128)} %pattern.1), custom_call_target="tpu_custom_call" | custom-call | tf_op jit(solution)/shard_map/pallas_call | solution.py:334
  2.4 1.0 copy-done
  3.3 4.7 %shard_map.105 = (bf16[736,768]{1,0:T(8,128)(2,1)S(1)}, bf16[736,768]{1,0:T(8,128)(2,1)S(1)}, f32[736,512]{1,0:T(8,128)S(1)}, f32[736,512]{1,0:T(8,128)S(1)}, f3...) custom-call(f32[120,729]{1,0:T(8,128)S(1)} %copy-done, ...), custom_call_target="tpu_custom_call" | custom-call | tf_op jit(solution)/shard_map/pallas_call | solution.py:342
  8.1 8.3 %shard_map.106 = (f32[736,128]{1,0:T(8,128)S(1)}, f32[8,128]{1,0:T(8,128)S(1)}, f32[128,768]{1,0:T(8,128)S(1)}) custom-call(bf16[736,768]{1,0:T(8,128)(2,1)S(1)} %get-tuple-element.37.khi, bf16[736,768]{1,0:T(8,128)(2,1)S(1)} %get-tuple-element.38.klo, f32[736,512]{1,0:T(8,128)S(1)} %get-tuple-element.39.hist, f32[736,512]{1,0:T(8,128)S(1)} %get-tuple-element.40.weight, ...), custom_call_target="tpu_custom_call" | custom-call | flops 3906994176 | bytes 1048576 | tf_op jit(solution)/shard_map/pallas_call | solution.py:373
  16.4 4.1 %collective-permute-start = (f32[128,768]{1,0:T(8,128)S(1)}, f32[128,768]{1,0:T(8,128)S(1)}, u32[]{:S(2)}, u32[]{:S(2)}) collective-permute-start(f32[128,768]{1,0:T(8,128)S(1)} %get-tuple-element.53), channel_id=1, source_target_pairs={{0,16},{1,17},{2,18},{3,19},{4,20},{5,21},{6,22},{7,23},{8,24},{9,... | collective-permute-start | bytes 1179656 | tf_op jit(solution)/shard_map/ppermute | solution.py:410
  20.5 8.4 %shard_map.107 = (f32[736,128]{1,0:T(8,128)S(1)}, f32[8,128]{1,0:T(8,128)S(1)}, f32[128,768]{1,0:T(8,128)S(1)}) custom-call(bf16[736,768]{1,0:T(8,128)(2,1)S(1)} %get-tuple-element.37.khi, bf16[736,768]{1,0:T(8,128)(2,1)S(1)} %get-tuple-element.38.klo, f32[736,512]{1,0:T(8,128)S(1)} %get-tuple-element.39.hist, f32[736,512]{1,0:T(8,128)S(1)} %get-tuple-element.40.weight, ...), custom_call_target="tpu_custom_call" | custom-call | flops 3906994176 | bytes 1048576 | tf_op jit(solution)/shard_map/pallas_call | solution.py:373
  28.9 1.6 %collective-permute-start.1 = (f32[128,768]{1,0:T(8,128)S(1)}, f32[128,768]{1,0:T(8,128)S(1)}, u32[]{:S(2)}, u32[]{:S(2)}) collective-permute-start(f32[128,768]{1,0:T(8,128)S(1)} %get-tuple-element.54), channel_id=1, source_target_pairs={{0,8},{1,9},{2,10},{3,11},{4,12},{5,13},{6,14},{7,15},{8,0},{9,1},... | collective-permute-start | bytes 1179656 | tf_op jit(solution)/shard_map/ppermute | solution.py:410
  30.6 8.7 %shard_map.108 = (f32[736,128]{1,0:T(8,128)S(1)}, f32[8,128]{1,0:T(8,128)S(1)}, f32[128,768]{1,0:T(8,128)S(1)}) custom-call(bf16[736,768]{1,0:T(8,128)(2,1)S(1)} %get-tuple-element.37.khi, bf16[736,768]{1,0:T(8,128)(2,1)S(1)} %get-tuple-element.38.klo, f32[736,512]{1,0:T(8,128)S(1)} %get-tuple-element.39.hist, f32[736,512]{1,0:T(8,128)S(1)} %get-tuple-element.40.weight, ...), custom_call_target="tpu_custom_call" | custom-call | flops 3906994176 | bytes 1048576 | tf_op jit(solution)/shard_map/pallas_call | solution.py:373
  39.3 0.1 collective-permute-start.2
  39.3 8.9 %shard_map.109 = (f32[736,128]{1,0:T(8,128)S(1)}, f32[8,128]{1,0:T(8,128)S(1)}, f32[128,768]{1,0:T(8,128)S(1)}) custom-call(bf16[736,768]{1,0:T(8,128)(2,1)S(1)} %get-tuple-element.37.khi, bf16[736,768]{1,0:T(8,128)(2,1)S(1)} %get-tuple-element.38.klo, f32[736,512]{1,0:T(8,128)S(1)} %get-tuple-element.39.hist, f32[736,512]{1,0:T(8,128)S(1)} %get-tuple-element.40.weight, ...), custom_call_target="tpu_custom_call" | custom-call | flops 3906994176 | bytes 1048576 | tf_op jit(solution)/shard_map/pallas_call | solution.py:373
  48.3 0.2 collective-permute-start.3
  48.5 3.1 %shard_map.110 = (f32[512,768]{1,0:T(8,128)}, f32[6,512]{1,0:T(8,128)}) custom-call(s32[8,512]{1,0:T(8,128)S(1)} %get-tuple-element.35.place, s32[8,512]{1,0:T(8,128)S(1)} %get-tuple-element.36.at, f32[736,128]{1,0:T(8,128)S(1)} %get-tuple-element.44.refs_0_, f32[736,128]{1,0:T(8,128)S(1)} %get-tuple-element.45.refs_1_, ...), custom_call_target="tpu_custom_call" | custom-call | flops 771751936 | bytes 1048576 | tf_op jit(solution)/shard_map/pallas_call | solution.py:396
  51.6 7.2 %all-to-all-start = ((f32[16,32,768]{2,1,0:T(8,128)}), f32[16,32,768]{2,1,0:T(8,128)}, u32[]{:S(2)}, u32[]{:S(2)}) async-start(f32[16,32,768]{2,1,0:T(8,128)} %bitcast.1), calls=%async_computation | async-start | bytes 3145728 | tf_op jit(solution)/shard_map/all_to_all | solution.py:413
  58.8 0.0 collective-permute-done.1.refs_1_
  58.8 0.7 collective-permute-done.2.refs_2_
  59.5 25.1 %collective-permute-done.3.refs_3_ = f32[128,768]{1,0:T(8,128)S(1)} collective-permute-done((f32[128,768]{1,0:T(8,128)S(1)}, f32[128,768]{1,0:T(8,128)S(1)}, u32[]{:S(2)}, u32[]{:S(2)}) %collective-permute-start.3) | collective-permute-done | bytes 393248 | tf_op jit(solution)/shard_map/ppermute | solution.py:410
  84.6 0.1 shard_map.111
  84.7 1.6 %collective-permute-start.4 = (f32[128,768]{1,0:T(8,128)S(1)}, f32[128,768]{1,0:T(8,128)S(1)}, u32[]{:S(2)}, u32[]{:S(2)}) collective-permute-start(f32[128,768]{1,0:T(8,128)S(1)} %get-tuple-element.64), channel_id=1, source_target_pairs={{0,2},{1,3},{2,0},{3,1},{4,6},{5,7},{6,4},{7,5},{8,10},{9,11},{10,... | collective-permute-start | bytes 1179656 | tf_op jit(solution)/shard_map/ppermute | solution.py:410
  86.3 1.5 %collective-permute-start.5 = (f32[128,768]{1,0:T(8,128)S(1)}, f32[128,768]{1,0:T(8,128)S(1)}, u32[]{:S(2)}, u32[]{:S(2)}) collective-permute-start(f32[128,768]{1,0:T(8,128)S(1)} %get-tuple-element.65), channel_id=1, source_target_pairs={{0,4},{1,5},{2,6},{3,7},{4,0},{5,1},{6,2},{7,3},{8,12},{9,13},{10,... | collective-permute-start | bytes 1179656 | tf_op jit(solution)/shard_map/ppermute | solution.py:410
  87.8 0.5 collective-permute-start.6
  88.3 8.5 %collective-permute-done.4.refs_1_ = f32[128,768]{1,0:T(8,128)S(1)} collective-permute-done((f32[128,768]{1,0:T(8,128)S(1)}, f32[128,768]{1,0:T(8,128)S(1)}, u32[]{:S(2)}, u32[]{:S(2)}) %collective-permute-start.4) | collective-permute-done | bytes 393248 | tf_op jit(solution)/shard_map/ppermute | solution.py:410
  96.8 8.8 %collective-permute-done.5.refs_2_ = f32[128,768]{1,0:T(8,128)S(1)} collective-permute-done((f32[128,768]{1,0:T(8,128)S(1)}, f32[128,768]{1,0:T(8,128)S(1)}, u32[]{:S(2)}, u32[]{:S(2)}) %collective-permute-start.5) | collective-permute-done | bytes 393248 | tf_op jit(solution)/shard_map/ppermute | solution.py:410
  105.6 0.0 collective-permute-done.6.refs_3_
  105.6 3.3 %shard_map.112 = f32[729,1024]{1,0:T(8,128)} custom-call(f32[512,768]{1,0:T(8,128)} %bitcast.2.pair, f32[128,768]{1,0:T(8,128)S(1)} %get-tuple-element.63.refs_0_, f32[128,768]{1,0:T(8,128)S(1)} %collective-permute-done.4.refs_1_, f32[128,768]{1,0:T(8,128)S(1)} %collective-permute-done.5.refs_2_, f32[128,768]{1,0:T(8,128)S(1)} %collective-permute-done.6.refs_3_), custom_call_target="tpu_custom_call" | custom-call | tf_op jit(solution)/shard_map/pallas_call | solution.py:432
  (3 shorter events, 0.0 us)
Async XLA Ops:
  2.4 1.0 copy-start
  16.4 42.4 %collective-permute-start = (f32[128,768]{1,0:T(8,128)S(1)}, f32[128,768]{1,0:T(8,128)S(1)}, u32[]{:S(2)}, u32[]{:S(2)}) collective-permute-start(f32[128,768]{1,0:T(8,128)S(1)} %get-tuple-element.53), channel_id=1, source_target_pairs={{0,16},{1,17},{2,18},{3,19},{4,20},{5,21},{6,22},{7,23},{8,24},{9,... | collective-permute-start | bytes 1179656 | tf_op jit(solution)/shard_map/ppermute | solution.py:410
  28.9 29.9 %collective-permute-start.1 = (f32[128,768]{1,0:T(8,128)S(1)}, f32[128,768]{1,0:T(8,128)S(1)}, u32[]{:S(2)}, u32[]{:S(2)}) collective-permute-start(f32[128,768]{1,0:T(8,128)S(1)} %get-tuple-element.54), channel_id=1, source_target_pairs={{0,8},{1,9},{2,10},{3,11},{4,12},{5,13},{6,14},{7,15},{8,0},{9,1},... | collective-permute-start | bytes 1179656 | tf_op jit(solution)/shard_map/ppermute | solution.py:410
  39.3 20.3 %collective-permute-start.2 = (f32[128,768]{1,0:T(8,128)S(1)}, f32[128,768]{1,0:T(8,128)S(1)}, u32[]{:S(2)}, u32[]{:S(2)}) collective-permute-start(f32[128,768]{1,0:T(8,128)S(1)} %get-tuple-element.57), channel_id=1, source_target_pairs={{0,17},{1,16},{2,19},{3,18},{4,21},{5,20},{6,23},{7,22},{8,25},{9,... | collective-permute-start | bytes 1179656 | tf_op jit(solution)/shard_map/ppermute | solution.py:410
  48.3 36.4 %collective-permute-start.3 = (f32[128,768]{1,0:T(8,128)S(1)}, f32[128,768]{1,0:T(8,128)S(1)}, u32[]{:S(2)}, u32[]{:S(2)}) collective-permute-start(f32[128,768]{1,0:T(8,128)S(1)} %get-tuple-element.60), channel_id=1, source_target_pairs={{0,9},{1,8},{2,11},{3,10},{4,13},{5,12},{6,15},{7,14},{8,1},{9,0},... | collective-permute-start | bytes 1179656 | tf_op jit(solution)/shard_map/ppermute | solution.py:410
  51.6 54.0 %all-to-all-start = ((f32[16,32,768]{2,1,0:T(8,128)}), f32[16,32,768]{2,1,0:T(8,128)}, u32[]{:S(2)}, u32[]{:S(2)}) async-start(f32[16,32,768]{2,1,0:T(8,128)} %bitcast.1), calls=%async_computation | async-start | bytes 3145728 | tf_op jit(solution)/shard_map/all_to_all | solution.py:413
  84.7 12.0 %collective-permute-start.4 = (f32[128,768]{1,0:T(8,128)S(1)}, f32[128,768]{1,0:T(8,128)S(1)}, u32[]{:S(2)}, u32[]{:S(2)}) collective-permute-start(f32[128,768]{1,0:T(8,128)S(1)} %get-tuple-element.64), channel_id=1, source_target_pairs={{0,2},{1,3},{2,0},{3,1},{4,6},{5,7},{6,4},{7,5},{8,10},{9,11},{10,... | collective-permute-start | bytes 1179656 | tf_op jit(solution)/shard_map/ppermute | solution.py:410
  86.3 19.3 %collective-permute-start.5 = (f32[128,768]{1,0:T(8,128)S(1)}, f32[128,768]{1,0:T(8,128)S(1)}, u32[]{:S(2)}, u32[]{:S(2)}) collective-permute-start(f32[128,768]{1,0:T(8,128)S(1)} %get-tuple-element.65), channel_id=1, source_target_pairs={{0,4},{1,5},{2,6},{3,7},{4,0},{5,1},{6,2},{7,3},{8,12},{9,13},{10,... | collective-permute-start | bytes 1179656 | tf_op jit(solution)/shard_map/ppermute | solution.py:410
  87.8 17.8 %collective-permute-start.6 = (f32[128,768]{1,0:T(8,128)S(1)}, f32[128,768]{1,0:T(8,128)S(1)}, u32[]{:S(2)}, u32[]{:S(2)}) collective-permute-start(f32[128,768]{1,0:T(8,128)S(1)} %get-tuple-element.66), channel_id=1, source_target_pairs={{0,6},{1,7},{2,4},{3,5},{4,2},{5,3},{6,0},{7,1},{8,14},{9,15},{10,... | collective-permute-start | bytes 1179656 | tf_op jit(solution)/shard_map/ppermute | solution.py:410

commit v3 on v2

--- a/solution.py
+++ b/solution.py
@@ -229,8 +229,11 @@
         image[r, 0:span] = pushed if c == 0 else image[r, 0:span] + pushed
         keep(r, c, (1.5 - weight[r, :]) * x)
     updated[...] = hist[...] + weight[...] * image[:, 0:span]
-    sent = blocks[0]
-    put(sent, 0, placed_rows(first, sent.shape[0], place, [*earlier_updated, updated]))
+    top, count = 0, sum(block.shape[0] for block in blocks)
+    sent = placed_rows(first, count, place, [*earlier_updated, updated])
+    for block in blocks:
+        put(block, 0, sent[top:top + block.shape[0]])
+        top += block.shape[0]
     out = s
     for c in range(comps):
         cpl = cstack[c].astype(jnp.bfloat16)
@@ -272,7 +275,7 @@
 
 
 def join_kernel(cap, *refs):
-    landed, blocks = refs[:4], refs[4:]
+    landed, blocks = refs[:3], refs[3:]
     for i, block in enumerate(blocks):
         for k, rows in enumerate(landed):
             block[k * cap:(k + 1) * cap, :] = rows[i * cap:(i + 1) * cap, :]
@@ -308,8 +311,11 @@
     for i, apart in enumerate((2, 1)):
         for k in range(lanes):
             at = pl.multiple_of((lane ^ k) * cap, cap)
-            top = (2 * (k % 2) + i) * cap
-            gather[i, pl.ds(at, cap), :] = blocks[k // 2][top:top + cap, :]
+            if i == 1 and k % 2 == 1:
+                gather[i, pl.ds(at, cap), :] = blocks[lanes // 2 + k // 2][...]
+            else:
+                top = (2 * (k % 2) + i) * cap
+                gather[i, pl.ds(at, cap), :] = blocks[k // 2][top:top + cap, :]
         copies += land_group(gather.at[i], 2, plane ^ apart, out, stage, sem, 4 + 2 * i)
     for copy in copies:
         copy.wait()
@@ -361,6 +367,7 @@
     )(*inputs)
 
     lanes = devices // PLANES
+    half = lanes // 2
     group = lanes * per_peer
     block = lambda height: jax.ShapeDtypeStruct((height, deep), f32)
     whole = lambda shape: pl.BlockSpec(shape, lambda i: (0,) * len(shape))
@@ -369,7 +376,7 @@
     for span in (LANES,) * (columns // LANES):
         part = lambda height: pl.BlockSpec((height, span), lambda i, at=left // span: (0, at))
         wide = comps * span
-        outs = [block(LANES)]
+        outs = [block(LANES)] if len(updated) < 3 else [block(per_peer)] * half
         done = pl.pallas_call(
             functools.partial(solve_kernel, 1.0 / math.sqrt(comps * nodes), left, len(updated)),
             grid=(1,),
@@ -391,7 +398,7 @@
         )(khi, klo, hist_s, weight_s, strain_s, cstack, pdir, place_s, *updated)
         updated.append(done[0])
         stress_s.append(done[1])
-        ready.extend(done[2:])
+        ready.append(done[2:])
         left += span
     pair, stress_out = pl.pallas_call(
         functools.partial(ship_kernel, devices, 2 * group, len(updated)),
@@ -409,35 +416,36 @@
     def hop(sent, mask):
         return lax.ppermute(sent, axes, [(s, s ^ mask) for s in range(devices)])
 
+    pair, *straight = lax.optimization_barrier((pair, *ready[-1]))
     planes = [list(range(z * lanes, (z + 1) * lanes)) for z in range(PLANES)]
     pair = lax.all_to_all(
         pair.reshape(2 * lanes, per_peer, deep), axes, split_axis=0, concat_axis=0, tiled=True,
         axis_index_groups=[planes[0] + planes[3], planes[1] + planes[2]],
     ).reshape(2 * group, deep)
-    hops = (2 * lanes, lanes, 2 * lanes + 1, lanes + 1)
+    hops = (2 * lanes, lanes, 2 * lanes + 1)
     landed = []
-    for sent, mask in zip(ready, hops):
+    for (sent,), mask in zip(ready, hops):
         landed.append(hop(sent, mask))
         landed[-2:] = lax.optimization_barrier(tuple(landed[-2:]))
-    half = lanes // 2
     joined = pl.pallas_call(
         functools.partial(join_kernel, per_peer),
-        out_shape=(block(4 * per_peer),) * half,
-        in_specs=[vmem] * 4,
+        out_shape=(block(3 * per_peer),) * half,
+        in_specs=[vmem] * 3,
         out_specs=[vmem] * half,
         compiler_params=params(),
         cost_estimate=pl.CostEstimate(flops=2**40, bytes_accessed=2**20, transcendentals=0),
     )(*landed)
     joined = [sent if i == 0 else hop(sent, 2 * i) for i, sent in enumerate(joined)]
+    direct = [hop(sent, lanes + 2 * i + 1) for i, sent in enumerate(straight)]
     new_history = pl.pallas_call(
         functools.partial(land_kernel, devices, per_peer),
         out_shape=jax.ShapeDtypeStruct((nodes, devices * per_peer), f32),
-        in_specs=[vmem] * (1 + half),
+        in_specs=[vmem] * (1 + 2 * half),
         out_specs=pl.BlockSpec(memory_space=pl.ANY),
         scratch_shapes=[pltpu.VMEM((8, nodes, LANES), f32), pltpu.SemaphoreType.DMA((8,)),
                         pltpu.VMEM((2, group, deep), f32)],
         compiler_params=params(),
-    )(pair, *joined)
+    )(pair, *joined, *direct)
     return (new_history, stress_out)
 
 

time: 111 us -> 99.4 us (0.90); the launches traced: 109 us -> 99.1 us
  waiting for transfers between devices: 43.1 us -> 29 us
  starting transfers between devices: 16.8 us -> 20.9 us
    ppermute x7 -> x10, waiting for transfers between devices: 43.1 us -> 29 us  [hop(): return lax.ppermute(sent, axes, [(s, s ^ mask) for s in range(devices)])]
    ppermute x7 -> x10, starting transfers between devices: 9.59 us -> 15.1 us  [hop(): return lax.ppermute(sent, axes, [(s, s ^ mask) for s in range(devices)])]
    all_to_all x1, starting transfers between devices: 7.23 us -> 5.82 us  [shards(): lax.all_to_all(pair.reshape(2 * lanes, per_peer, deep), axes, split_axis=...]
  transfers between devices with their start and end apart: 8 -> 11, of which waited for: 4 -> 6; matrix products, arithmetic and copies ran while one was open for 0% -> 0% of each run, Pallas kernels for 27% -> 29%
where the time goes in v3:
time: 99.4 us; the launch traced here: 99.1 us
  Pallas kernels  47.3 us (48%)
  waiting for transfers between devices  29 us (29%)
  starting transfers between devices  20.9 us (21%)
    pallas_call x4, Pallas kernels, shards(): pl.pallas_call(functools.partial(solve_kernel, 1.0 / math.sqrt(comps * no...  34.4 us
    ppermute x10, waiting for transfers between devices, hop(): return lax.ppermute(sent, axes, [(s, s ^ mask) for s in range(devices)])  29 us
    ppermute x10, starting transfers between devices, hop(): return lax.ppermute(sent, axes, [(s, s ^ mask) for s in range(devices)])  15.1 us
    all_to_all x1, starting transfers between devices, shards(): lax.all_to_all(pair.reshape(2 * lanes, per_peer, deep), axes, split_axis=...  5.82 us
    pallas_call x1, Pallas kernels, shards(): pl.pallas_call(functools.partial(prep_kernel, devices, per_peer, comps, v...  4.72 us
    pallas_call x1, Pallas kernels, shards(): pl.pallas_call(functools.partial(land_kernel, devices, per_peer), out_sha...  3.27 us
    pallas_call x1, Pallas kernels, shards(): pl.pallas_call(functools.partial(ship_kernel, devices, 2 * group, len(upd...  3.09 us
  transfers between devices with their start and end apart: 11, of which 6 were waited for; matrix products, arithmetic and copies ran while one was open for 0% of the time, Pallas kernels for 29%

profile of v3, /device:TPU:0, one launch (start us, length us, event | category | flops | bytes accessed | tf_op | source)
XLA Modules:
  0.0 99.1 jit_solution(11847414649476640209)
XLA Ops:
  0.6 1.7 %shard_map.104.refs_0_ = f32[120,729]{1,0:T(8,128)} custom-call(f32[3,6,729]{2,1,0:T(8,128)} %coupling.1, f32[3,729]{1,0:T(4,128)} %plastic.1, f32[6,512]{1,0:T(8,128)} %strain.1, s32[1,512]{1,0:T(1,128)} %bitcast.3, s32[1,512]{1,0:T(1,128)} %qp.1, s32[9,9]{1,0:T(8,128)} %pattern.1), custom_call_target="tpu_custom_call" | custom-call | tf_op jit(solution)/shard_map/pallas_call | solution.py:340
  2.4 1.0 copy-done
  3.3 4.7 %shard_map.105 = (bf16[736,768]{1,0:T(8,128)(2,1)S(1)}, bf16[736,768]{1,0:T(8,128)(2,1)S(1)}, f32[736,512]{1,0:T(8,128)S(1)}, f32[736,512]{1,0:T(8,128)S(1)}, f3...) custom-call(f32[120,729]{1,0:T(8,128)S(1)} %copy-done, ...), custom_call_target="tpu_custom_call" | custom-call | tf_op jit(solution)/shard_map/pallas_call | solution.py:348
  8.1 8.3 %shard_map.106 = (f32[736,128]{1,0:T(8,128)S(1)}, f32[8,128]{1,0:T(8,128)S(1)}, f32[128,768]{1,0:T(8,128)S(1)}) custom-call(bf16[736,768]{1,0:T(8,128)(2,1)S(1)} %get-tuple-element.43.khi, bf16[736,768]{1,0:T(8,128)(2,1)S(1)} %get-tuple-element.44.klo, f32[736,512]{1,0:T(8,128)S(1)} %get-tuple-element.45.hist, f32[736,512]{1,0:T(8,128)S(1)} %get-tuple-element.46.weight, ...), custom_call_target="tpu_custom_call" | custom-call | flops 3906994176 | bytes 1048576 | tf_op jit(solution)/shard_map/pallas_call | solution.py:380
  16.4 4.1 %collective-permute-start = (f32[128,768]{1,0:T(8,128)S(1)}, f32[128,768]{1,0:T(8,128)S(1)}, u32[]{:S(2)}, u32[]{:S(2)}) collective-permute-start(f32[128,768]{1,0:T(8,128)S(1)} %get-tuple-element.64), channel_id=1, source_target_pairs={{0,16},{1,17},{2,18},{3,19},{4,20},{5,21},{6,22},{7,23},{8,24},{9,... | collective-permute-start | bytes 1179656 | tf_op jit(solution)/shard_map/ppermute | solution.py:417
  20.5 8.4 %shard_map.107 = (f32[736,128]{1,0:T(8,128)S(1)}, f32[8,128]{1,0:T(8,128)S(1)}, f32[128,768]{1,0:T(8,128)S(1)}) custom-call(bf16[736,768]{1,0:T(8,128)(2,1)S(1)} %get-tuple-element.43.khi, bf16[736,768]{1,0:T(8,128)(2,1)S(1)} %get-tuple-element.44.klo, f32[736,512]{1,0:T(8,128)S(1)} %get-tuple-element.45.hist, f32[736,512]{1,0:T(8,128)S(1)} %get-tuple-element.46.weight, ...), custom_call_target="tpu_custom_call" | custom-call | flops 3906994176 | bytes 1048576 | tf_op jit(solution)/shard_map/pallas_call | solution.py:380
  28.9 1.6 %collective-permute-start.1 = (f32[128,768]{1,0:T(8,128)S(1)}, f32[128,768]{1,0:T(8,128)S(1)}, u32[]{:S(2)}, u32[]{:S(2)}) collective-permute-start(f32[128,768]{1,0:T(8,128)S(1)} %get-tuple-element.65), channel_id=1, source_target_pairs={{0,8},{1,9},{2,10},{3,11},{4,12},{5,13},{6,14},{7,15},{8,0},{9,1},... | collective-permute-start | bytes 1179656 | tf_op jit(solution)/shard_map/ppermute | solution.py:417
  30.6 8.7 %shard_map.108 = (f32[736,128]{1,0:T(8,128)S(1)}, f32[8,128]{1,0:T(8,128)S(1)}, f32[128,768]{1,0:T(8,128)S(1)}) custom-call(bf16[736,768]{1,0:T(8,128)(2,1)S(1)} %get-tuple-element.43.khi, bf16[736,768]{1,0:T(8,128)(2,1)S(1)} %get-tuple-element.44.klo, f32[736,512]{1,0:T(8,128)S(1)} %get-tuple-element.45.hist, f32[736,512]{1,0:T(8,128)S(1)} %get-tuple-element.46.weight, ...), custom_call_target="tpu_custom_call" | custom-call | flops 3906994176 | bytes 1048576 | tf_op jit(solution)/shard_map/pallas_call | solution.py:380
  39.3 8.9 %shard_map.109 = (f32[736,128]{1,0:T(8,128)S(1)}, f32[8,128]{1,0:T(8,128)S(1)}, f32[32,768]{1,0:T(8,128)S(1)}, f32[32,768]{1,0:T(8,128)S(1)}, f32[32,768]{1,0:T(8,128)S(1)}, /*index=5*/f32[32,768]{1,0:T(8,128)S(1)}) custom-call(bf16[736,768]{1,0:T(8,128)(2,1)S(1)} %get-tuple-element.43.khi, bf16[736,768]{1,0:T(8,128)(2,1)S(1)} %get-tuple-element.44.klo, ...), custom_call_target="tpu_custom_call" | custom-call | flops 3906994176 | bytes 1048576 | tf_op jit(solution)/shard_map/pallas_call | solution.py:380
  48.3 3.1 %shard_map.110 = (f32[512,768]{1,0:T(8,128)}, f32[6,512]{1,0:T(8,128)}) custom-call(s32[8,512]{1,0:T(8,128)S(1)} %get-tuple-element.41.place, s32[8,512]{1,0:T(8,128)S(1)} %get-tuple-element.42.at, f32[736,128]{1,0:T(8,128)S(1)} %get-tuple-element.50.refs_0_, f32[736,128]{1,0:T(8,128)S(1)} %get-tuple-element.51.refs_1_, ...), custom_call_target="tpu_custom_call" | custom-call | flops 771751936 | bytes 1048576 | tf_op jit(solution)/shard_map/pallas_call | solution.py:403
  51.4 5.8 %all-to-all-start = ((f32[16,32,768]{2,1,0:T(8,128)}), f32[16,32,768]{2,1,0:T(8,128)}, u32[]{:S(2)}, u32[]{:S(2)}) async-start(f32[16,32,768]{2,1,0:T(8,128)} %bitcast.1), calls=%async_computation | async-start | bytes 3145728 | tf_op jit(solution)/shard_map/all_to_all | solution.py:421
  57.2 2.2 %collective-permute-done.2.refs_2_ = f32[128,768]{1,0:T(8,128)S(1)} collective-permute-done((f32[128,768]{1,0:T(8,128)S(1)}, f32[128,768]{1,0:T(8,128)S(1)}, u32[]{:S(2)}, u32[]{:S(2)}) %collective-permute-start.2) | collective-permute-done | bytes 393248 | tf_op jit(solution)/shard_map/ppermute | solution.py:417
  59.5 1.6 %collective-permute-start.3 = (f32[96,768]{1,0:T(8,128)S(1)}, f32[96,768]{1,0:T(8,128)S(1)}, u32[]{:S(2)}, u32[]{:S(2)}) collective-permute-start(f32[96,768]{1,0:T(8,128)S(1)} %get-tuple-element.72), channel_id=1, source_target_pairs={{0,2},{1,3},{2,0},{3,1},{4,6},{5,7},{6,4},{7,5},{8,10},{9,11},{10,... | collective-permute-start | bytes 884744 | tf_op jit(solution)/shard_map/ppermute | solution.py:417
  61.0 1.5 %collective-permute-start.4 = (f32[96,768]{1,0:T(8,128)S(1)}, f32[96,768]{1,0:T(8,128)S(1)}, u32[]{:S(2)}, u32[]{:S(2)}) collective-permute-start(f32[96,768]{1,0:T(8,128)S(1)} %get-tuple-element.73), channel_id=1, source_target_pairs={{0,4},{1,5},{2,6},{3,7},{4,0},{5,1},{6,2},{7,3},{8,12},{9,13},{10,... | collective-permute-start | bytes 884744 | tf_op jit(solution)/shard_map/ppermute | solution.py:417
  62.6 0.5 collective-permute-start.5
  63.0 2.7 %collective-permute-start.7 = (f32[32,768]{1,0:T(8,128)S(1)}, f32[32,768]{1,0:T(8,128)S(1)}, u32[]{:S(2)}, u32[]{:S(2)}) collective-permute-start(f32[32,768]{1,0:T(8,128)S(1)} %get-tuple-element.76), channel_id=1, source_target_pairs={{0,11},{1,10},{2,9},{3,8},{4,15},{5,14},{6,13},{7,12},{8,3},{9,2},... | collective-permute-start | bytes 294920 | tf_op jit(solution)/shard_map/ppermute | solution.py:417
  65.7 15.5 %collective-permute-done.6.refs_4_ = f32[32,768]{1,0:T(8,128)S(1)} collective-permute-done((f32[32,768]{1,0:T(8,128)S(1)}, f32[32,768]{1,0:T(8,128)S(1)}, u32[]{:S(2)}, u32[]{:S(2)}) %collective-permute-start.6) | collective-permute-done | bytes 98336 | tf_op jit(solution)/shard_map/ppermute | solution.py:417
  81.2 1.4 %collective-permute-start.8 = (f32[32,768]{1,0:T(8,128)S(1)}, f32[32,768]{1,0:T(8,128)S(1)}, u32[]{:S(2)}, u32[]{:S(2)}) collective-permute-start(f32[32,768]{1,0:T(8,128)S(1)} %get-tuple-element.77), channel_id=1, source_target_pairs={{0,13},{1,12},{2,15},{3,14},{4,9},{5,8},{6,11},{7,10},{8,5},{9,4},... | collective-permute-start | bytes 294920 | tf_op jit(solution)/shard_map/ppermute | solution.py:417
  82.6 1.6 %collective-permute-done.7.refs_5_ = f32[32,768]{1,0:T(8,128)S(1)} collective-permute-done((f32[32,768]{1,0:T(8,128)S(1)}, f32[32,768]{1,0:T(8,128)S(1)}, u32[]{:S(2)}, u32[]{:S(2)}) %collective-permute-start.7) | collective-permute-done | bytes 98336 | tf_op jit(solution)/shard_map/ppermute | solution.py:417
  84.2 1.6 %collective-permute-start.9 = (f32[32,768]{1,0:T(8,128)S(1)}, f32[32,768]{1,0:T(8,128)S(1)}, u32[]{:S(2)}, u32[]{:S(2)}) collective-permute-start(f32[32,768]{1,0:T(8,128)S(1)} %get-tuple-element.78), channel_id=1, source_target_pairs={{0,15},{1,14},{2,13},{3,12},{4,11},{5,10},{6,9},{7,8},{8,7},{9,6},... | collective-permute-start | bytes 294920 | tf_op jit(solution)/shard_map/ppermute | solution.py:417
  85.9 1.5 %collective-permute-done.8.refs_6_ = f32[32,768]{1,0:T(8,128)S(1)} collective-permute-done((f32[32,768]{1,0:T(8,128)S(1)}, f32[32,768]{1,0:T(8,128)S(1)}, u32[]{:S(2)}, u32[]{:S(2)}) %collective-permute-start.8) | collective-permute-done | bytes 98336 | tf_op jit(solution)/shard_map/ppermute | solution.py:417
  87.4 3.7 %collective-permute-done.9.refs_7_ = f32[32,768]{1,0:T(8,128)S(1)} collective-permute-done((f32[32,768]{1,0:T(8,128)S(1)}, f32[32,768]{1,0:T(8,128)S(1)}, u32[]{:S(2)}, u32[]{:S(2)}) %collective-permute-start.9) | collective-permute-done | bytes 98336 | tf_op jit(solution)/shard_map/ppermute | solution.py:417
  91.1 4.5 %collective-permute-done.5.refs_3_ = f32[96,768]{1,0:T(8,128)S(1)} collective-permute-done((f32[96,768]{1,0:T(8,128)S(1)}, f32[96,768]{1,0:T(8,128)S(1)}, u32[]{:S(2)}, u32[]{:S(2)}) %collective-permute-start.5) | collective-permute-done | bytes 294944 | tf_op jit(solution)/shard_map/ppermute | solution.py:417
  95.6 3.3 %shard_map.112 = f32[729,1024]{1,0:T(8,128)} custom-call(f32[512,768]{1,0:T(8,128)} %bitcast.2.pair, f32[96,768]{1,0:T(8,128)S(1)} %get-tuple-element.71.refs_0_, f32[96,768]{1,0:T(8,128)S(1)} %collective-permute-done.3.refs_1_, f32[96,768]{1,0:T(8,128)S(1)} %collective-permute-done.4.refs_2_, f32[96,768]{1,0:T(8,128)S(1)} %collective-permute-done.5.refs_3_, ...), custom_call_target="tpu_custom_call" | custom-call | tf_op jit(solution)/shard_map/pallas_call | solution.py:440
  (9 shorter events, 0.2 us)
Async XLA Ops:
  2.4 1.0 copy-start
  16.4 40.8 %collective-permute-start = (f32[128,768]{1,0:T(8,128)S(1)}, f32[128,768]{1,0:T(8,128)S(1)}, u32[]{:S(2)}, u32[]{:S(2)}) collective-permute-start(f32[128,768]{1,0:T(8,128)S(1)} %get-tuple-element.64), channel_id=1, source_target_pairs={{0,16},{1,17},{2,18},{3,19},{4,20},{5,21},{6,22},{7,23},{8,24},{9,... | collective-permute-start | bytes 1179656 | tf_op jit(solution)/shard_map/ppermute | solution.py:417
  28.9 28.3 %collective-permute-start.1 = (f32[128,768]{1,0:T(8,128)S(1)}, f32[128,768]{1,0:T(8,128)S(1)}, u32[]{:S(2)}, u32[]{:S(2)}) collective-permute-start(f32[128,768]{1,0:T(8,128)S(1)} %get-tuple-element.65), channel_id=1, source_target_pairs={{0,8},{1,9},{2,10},{3,11},{4,12},{5,13},{6,14},{7,15},{8,0},{9,1},... | collective-permute-start | bytes 1179656 | tf_op jit(solution)/shard_map/ppermute | solution.py:417
  39.3 20.1 %collective-permute-start.2 = (f32[128,768]{1,0:T(8,128)S(1)}, f32[128,768]{1,0:T(8,128)S(1)}, u32[]{:S(2)}, u32[]{:S(2)}) collective-permute-start(f32[128,768]{1,0:T(8,128)S(1)} %get-tuple-element.68), channel_id=1, source_target_pairs={{0,17},{1,16},{2,19},{3,18},{4,21},{5,20},{6,23},{7,22},{8,25},{9,... | collective-permute-start | bytes 1179656 | tf_op jit(solution)/shard_map/ppermute | solution.py:417
  51.4 44.3 %all-to-all-start = ((f32[16,32,768]{2,1,0:T(8,128)}), f32[16,32,768]{2,1,0:T(8,128)}, u32[]{:S(2)}, u32[]{:S(2)}) async-start(f32[16,32,768]{2,1,0:T(8,128)} %bitcast.1), calls=%async_computation | async-start | bytes 3145728 | tf_op jit(solution)/shard_map/all_to_all | solution.py:421
  59.5 31.6 %collective-permute-start.3 = (f32[96,768]{1,0:T(8,128)S(1)}, f32[96,768]{1,0:T(8,128)S(1)}, u32[]{:S(2)}, u32[]{:S(2)}) collective-permute-start(f32[96,768]{1,0:T(8,128)S(1)} %get-tuple-element.72), channel_id=1, source_target_pairs={{0,2},{1,3},{2,0},{3,1},{4,6},{5,7},{6,4},{7,5},{8,10},{9,11},{10,... | collective-permute-start | bytes 884744 | tf_op jit(solution)/shard_map/ppermute | solution.py:417
  61.0 30.1 %collective-permute-start.4 = (f32[96,768]{1,0:T(8,128)S(1)}, f32[96,768]{1,0:T(8,128)S(1)}, u32[]{:S(2)}, u32[]{:S(2)}) collective-permute-start(f32[96,768]{1,0:T(8,128)S(1)} %get-tuple-element.73), channel_id=1, source_target_pairs={{0,4},{1,5},{2,6},{3,7},{4,0},{5,1},{6,2},{7,3},{8,12},{9,13},{10,... | collective-permute-start | bytes 884744 | tf_op jit(solution)/shard_map/ppermute | solution.py:417
  62.6 33.1 %collective-permute-start.5 = (f32[96,768]{1,0:T(8,128)S(1)}, f32[96,768]{1,0:T(8,128)S(1)}, u32[]{:S(2)}, u32[]{:S(2)}) collective-permute-start(f32[96,768]{1,0:T(8,128)S(1)} %get-tuple-element.74), channel_id=1, source_target_pairs={{0,6},{1,7},{2,4},{3,5},{4,2},{5,3},{6,0},{7,1},{8,14},{9,15},{10,... | collective-permute-start | bytes 884744 | tf_op jit(solution)/shard_map/ppermute | solution.py:417
  63.0 18.2 %collective-permute-start.6 = (f32[32,768]{1,0:T(8,128)S(1)}, f32[32,768]{1,0:T(8,128)S(1)}, u32[]{:S(2)}, u32[]{:S(2)}) collective-permute-start(f32[32,768]{1,0:T(8,128)S(1)} %get-tuple-element.75), channel_id=1, source_target_pairs={{0,9},{1,8},{2,11},{3,10},{4,13},{5,12},{6,15},{7,14},{8,1},{9,0},... | collective-permute-start | bytes 294920 | tf_op jit(solution)/shard_map/ppermute | solution.py:417
  63.0 21.2 %collective-permute-start.7 = (f32[32,768]{1,0:T(8,128)S(1)}, f32[32,768]{1,0:T(8,128)S(1)}, u32[]{:S(2)}, u32[]{:S(2)}) collective-permute-start(f32[32,768]{1,0:T(8,128)S(1)} %get-tuple-element.76), channel_id=1, source_target_pairs={{0,11},{1,10},{2,9},{3,8},{4,15},{5,14},{6,13},{7,12},{8,3},{9,2},... | collective-permute-start | bytes 294920 | tf_op jit(solution)/shard_map/ppermute | solution.py:417
  81.2 6.2 %collective-permute-start.8 = (f32[32,768]{1,0:T(8,128)S(1)}, f32[32,768]{1,0:T(8,128)S(1)}, u32[]{:S(2)}, u32[]{:S(2)}) collective-permute-start(f32[32,768]{1,0:T(8,128)S(1)} %get-tuple-element.77), channel_id=1, source_target_pairs={{0,13},{1,12},{2,15},{3,14},{4,9},{5,8},{6,11},{7,10},{8,5},{9,4},... | collective-permute-start | bytes 294920 | tf_op jit(solution)/shard_map/ppermute | solution.py:417
  84.2 6.9 %collective-permute-start.9 = (f32[32,768]{1,0:T(8,128)S(1)}, f32[32,768]{1,0:T(8,128)S(1)}, u32[]{:S(2)}, u32[]{:S(2)}) collective-permute-start(f32[32,768]{1,0:T(8,128)S(1)} %get-tuple-element.78), channel_id=1, source_target_pairs={{0,15},{1,14},{2,13},{3,12},{4,11},{5,10},{6,9},{7,8},{8,7},{9,6},... | collective-permute-start | bytes 294920 | tf_op jit(solution)/shard_map/ppermute | solution.py:417
